TPU v7x, 32 devices: a whole 2x2x4 slice. The times are simulated.
32 devices in a mesh: dp: 16 (over z, y, x), rep: 2 (over core).
Axes of the slice: x: 2, y: 2, z: 4, core: 2. Of those that a mesh axis runs over, the one named last changes fastest.
Arguments:
- start_deter: bfloat16 [3072, 512], P(('dp', 'rep')), may hold values from -3 to 3
- frame_mask: int32 [3072], P(('dp', 'rep')), may hold values 0 or 1
- counts: int32 [32], P(('dp', 'rep')), may hold values from 0 to 96, as said below
- route: int32 [3072], P(('dp', 'rep')), may hold values from 0 to 767, as said below
- weights_flat: bfloat16 [4194304], P('dp'), may hold values from -3 to 3
- act_embed: bfloat16 [18, 512], replicated, may hold values from -2.5 to 2.5
- gru_gain: bfloat16 [1536], replicated, may hold values from 0.5 to 1.5
- gru_bias: bfloat16 [1536], replicated, may hold values from -1.5 to 1.5
- actor_head: bfloat16 [512, 18], replicated, may hold values from -0.75 to 0.75
- critic_head: bfloat16 [512], replicated, may hold values from -0.25 to 0.25
- latent_idx: int32 [1536, 16, 32], P(('dp', 'rep')), may hold values from 0 to 31
- action_idx: int32 [1536, 16], P(('dp', 'rep')), may hold values from 0 to 17
- rewards: float32 [1536, 16], P(('dp', 'rep')), may hold values from -12 to 12
Outputs:
- loss: float32 [], replicated
- start_grad: float32 [3072, 512], P(('dp', 'rep'))
- weights_grad: float32 [4194304], P('dp')
- embed_grad: float32 [18, 512], replicated
- gain_grad: float32 [1536], replicated
- bias_grad: float32 [1536], replicated
- actor_head_grad: float32 [512, 18], replicated
- critic_head_grad: float32 [512], replicated
Inputs may be any that keep to these rules, and one draw needn't show every extreme that they name: Within each index of rep, the counts of the 16 devices sum to 768, and some device holds 96. `route`: for slots below the device's count, the used slots of one rep index fill every position of every destination exactly once, and at most 12 slots of one device go to one destination, reached by some device; entries of other slots are arbitrary.
All inputs are finite; a program needn't handle non-finite values. No bound on the sum of `frame_mask` on one device may be relied on, other than what follows from the above.
Results may differ from a plain program's by a relative error of at most 0.0075.
Values may be sent and summed in bfloat16 or wider, within the bound.
A program may use at most 192 MiB of HBM per device.

v0:
```python
import jax
import jax.numpy as jnp
from jax import lax
from jax.sharding import PartitionSpec as P

DET = 512
CLASSES = 32
UNITS = 512
ACTIONS = 18
MICRO = 2
STOCH = 1024


discount = 0.99
entropy_weight = 0.1
norm_eps = 1e-05


def product(left, right):
    return jnp.dot(left, right, preferred_element_type=jnp.float32)


def product_t(left, right):
    return lax.dot_general(
        left, right, (((0,), (0,)), ((), ())), preferred_element_type=jnp.float32
    )


def product_nt(left, right):
    return lax.dot_general(
        left, right, (((1,), (1,)), ((), ())), preferred_element_type=jnp.float32
    )


def elu_grad(value):
    return jnp.where(value > 0, 1.0, jnp.exp(jnp.minimum(value, 0.0)))


def unpack(flat):
    shapes = [
        (STOCH, DET),
        (2 * DET, 3 * DET),
        (DET + STOCH, UNITS),
        (UNITS, UNITS),
        (DET + STOCH, UNITS),
        (UNITS, UNITS),
    ]
    pieces = []
    offset = 0
    for piece_shape in shapes:
        piece_size = piece_shape[0] * piece_shape[1]
        pieces.append(flat[offset : offset + piece_size].reshape(piece_shape))
        offset = offset + piece_size
    return tuple(pieces)


def gru_update(gru_raw, state, gain, bias):
    ln_mean = jnp.mean(gru_raw, axis=-1, keepdims=True)
    centred = gru_raw - ln_mean
    inv_std = lax.rsqrt(jnp.mean(centred * centred, axis=-1, keepdims=True) + norm_eps)
    normed = centred * inv_std
    parts = normed * gain + bias
    middle = parts[..., DET : 2 * DET]
    reset = jax.nn.sigmoid(parts[..., :DET])
    candidate = jnp.tanh(reset * middle)
    update = jax.nn.sigmoid(parts[..., 2 * DET :] - 1.0)
    new_state = update * candidate + (1.0 - update) * state
    return (new_state, (normed, inv_std, reset, candidate, update, middle))


def heads_forward(state_rows, latent_rows, first, second, head):
    hidden_one = product(state_rows, first[:DET]) + product(latent_rows, first[DET:])
    active_one = jax.nn.elu(hidden_one).astype(jnp.bfloat16)
    hidden_two = product(active_one, second)
    active_two = jax.nn.elu(hidden_two).astype(jnp.bfloat16)
    return ((hidden_one, active_one, hidden_two, active_two), product(active_two, head))


def heads_backward(state_rows, latent_rows, kept, first, second, head, grad_out):
    hidden_one, active_one, hidden_two, active_two = kept
    if head.ndim == 1:
        grad_head = product(grad_out, active_two)
        grad_two = grad_out.astype(jnp.float32)[:, None] * head.astype(jnp.float32)[None, :]
    else:
        grad_head = product_t(active_two, grad_out)
        grad_two = product_nt(grad_out, head)
    hidden_two_grad = (grad_two * elu_grad(hidden_two)).astype(jnp.bfloat16)
    grad_second = product_t(active_one, hidden_two_grad)
    grad_one = product_nt(hidden_two_grad, second)
    hidden_one_grad = (grad_one * elu_grad(hidden_one)).astype(jnp.bfloat16)
    grad_first = jnp.concatenate(
        [product_t(state_rows, hidden_one_grad), product_t(latent_rows, hidden_one_grad)], 0
    )
    grad_state = product_nt(hidden_one_grad, first[:DET])
    return (grad_first, grad_second, grad_head, grad_state)


def forward_micro(
    gathered, small_weights, start_h, latent_block, action_block, adv_block, mask_block
):
    win_z, w_gru, actor_one, actor_two, critic_one, critic_two = unpack(gathered)
    act_embed, gain, bias, actor_head, critic_head = small_weights
    horizon, starts_here = adv_block.shape

    def dyn_step(state, inputs):
        latent_now, action_now = inputs
        state_low = state.astype(jnp.bfloat16)
        pre_act = product(latent_now, win_z) + product(action_now, act_embed)
        input_low = jax.nn.elu(pre_act).astype(jnp.bfloat16)
        gru_raw = product(input_low, w_gru[:DET]) + product(state_low, w_gru[DET:])
        new_state = gru_update(gru_raw, state, gain, bias)[0]
        return (new_state, (state, pre_act, gru_raw))

    last_state, (states, pre_acts, gru_raws) = lax.scan(
        dyn_step, start_h, (latent_block[:-1], action_block[:-1])
    )
    all_states = jnp.concatenate([states, last_state[None]], 0)
    row_count = horizon * starts_here
    state_rows = all_states.astype(jnp.bfloat16).reshape(row_count, DET)
    latent_rows = latent_block.reshape(row_count, STOCH)
    actor_kept, logits = heads_forward(state_rows, latent_rows, actor_one, actor_two, actor_head)
    critic_kept, values = heads_forward(
        state_rows, latent_rows, critic_one, critic_two, critic_head
    )
    log_probs = jax.nn.log_softmax(logits, axis=-1)
    probs = jnp.exp(log_probs)
    action_rows = action_block.reshape(row_count, ACTIONS).astype(jnp.float32)
    chosen = jnp.sum(log_probs * action_rows, axis=-1)
    entropy = -jnp.sum(probs * log_probs, axis=-1)
    adv_rows = adv_block.reshape(row_count)
    row_weight = mask_block.reshape(row_count) / horizon
    loss_part = jnp.sum(
        row_weight
        * (-adv_rows * chosen - entropy_weight * entropy + 0.5 * (values - adv_rows) ** 2)
    )
    grad_logits = (
        row_weight[:, None]
        * (
            -adv_rows[:, None] * (action_rows - probs)
            + entropy_weight * probs * (log_probs + entropy[:, None])
        )
    ).astype(jnp.bfloat16)
    grad_values = (row_weight * (values - adv_rows)).astype(jnp.bfloat16)
    kept = (
        states,
        pre_acts,
        gru_raws,
        state_rows,
        latent_rows,
        actor_kept,
        critic_kept,
        grad_logits,
        grad_values,
    )
    return (kept, loss_part)


def backward_micro(gathered, small_weights, kept, latent_block, action_block):
    win_z, w_gru, actor_one, actor_two, critic_one, critic_two = unpack(gathered)
    act_embed, gain, bias, actor_head, critic_head = small_weights
    (
        states,
        pre_acts,
        gru_raws,
        state_rows,
        latent_rows,
        actor_kept,
        critic_kept,
        grad_logits,
        grad_values,
    ) = kept
    steps_minus, starts_here = (states.shape[0], states.shape[1])
    horizon = steps_minus + 1
    grad_a_one, grad_a_two, grad_a_head, state_from_actor = heads_backward(
        state_rows, latent_rows, actor_kept, actor_one, actor_two, actor_head, grad_logits
    )
    grad_c_one, grad_c_two, grad_c_head, state_from_critic = heads_backward(
        state_rows, latent_rows, critic_kept, critic_one, critic_two, critic_head, grad_values
    )
    state_grad = (state_from_actor + state_from_critic).reshape(horizon, starts_here, DET)

    def back_step(carry, inputs):
        state, pre_act, gru_raw, state_grad_now = inputs
        normed, inv_std, reset, candidate, update, middle = gru_update(gru_raw, state, gain, bias)[
            1
        ]
        update_grad = carry * (candidate - state)
        cand_grad = carry * update
        direct = carry * (1.0 - update)
        grad_third = update_grad * update * (1.0 - update)
        inner_grad = cand_grad * (1.0 - candidate * candidate)
        grad_second = inner_grad * reset
        grad_first = inner_grad * middle * reset * (1.0 - reset)
        part_grad = jnp.concatenate([grad_first, grad_second, grad_third], -1)
        gain_part = jnp.sum(part_grad * normed, axis=0)
        bias_part = jnp.sum(part_grad, axis=0)
        normed_grad = part_grad * gain
        raw_grad = inv_std * (
            normed_grad
            - jnp.mean(normed_grad, axis=-1, keepdims=True)
            - normed * jnp.mean(normed_grad * normed, axis=-1, keepdims=True)
        )
        raw_low = raw_grad.astype(jnp.bfloat16)
        input_grad = product_nt(raw_low, w_gru[:DET])
        state_from = product_nt(raw_low, w_gru[DET:])
        pre_low = (input_grad * elu_grad(pre_act)).astype(jnp.bfloat16)
        return (direct + state_from + state_grad_now, (raw_low, pre_low, gain_part, bias_part))

    start_grad, (raw_grads, pre_grads, gain_parts, bias_parts) = lax.scan(
        back_step, state_grad[-1], (states, pre_acts, gru_raws, state_grad[:-1]), reverse=True
    )
    step_rows = steps_minus * starts_here
    input_rows = jax.nn.elu(pre_acts).astype(jnp.bfloat16).reshape(step_rows, DET)
    state_lows = states.astype(jnp.bfloat16).reshape(step_rows, DET)
    raw_rows = raw_grads.reshape(step_rows, 3 * DET)
    pre_rows = pre_grads.reshape(step_rows, DET)
    grad_gru = jnp.concatenate(
        [product_t(input_rows, raw_rows), product_t(state_lows, raw_rows)], 0
    )
    grad_win = product_t(latent_block[:-1].reshape(step_rows, STOCH), pre_rows)
    grad_embed = product_t(action_block[:-1].reshape(step_rows, ACTIONS), pre_rows)
    flat_grad = jnp.concatenate(
        [
            piece.reshape(-1)
            for piece in (grad_win, grad_gru, grad_a_one, grad_a_two, grad_c_one, grad_c_two)
        ]
    )
    small_grads = (
        grad_embed,
        jnp.sum(gain_parts, axis=0),
        jnp.sum(bias_parts, axis=0),
        grad_a_head,
        grad_c_head,
    )
    return (flat_grad, small_grads, start_grad)


def on_device(
    start_deter,
    frame_mask,
    counts,
    route,
    weights_flat,
    act_embed,
    gru_gain,
    gru_bias,
    actor_head,
    critic_head,
    latent_idx,
    action_idx,
    rewards,
):
    devices = lax.axis_size("dp")
    slots = start_deter.shape[0]
    capacity = latent_idx.shape[0]
    horizon = latent_idx.shape[1]
    pairs = max(2, 2 * slots // devices)
    lanes = devices * pairs
    slot_ids = jnp.arange(slots, dtype=jnp.int32)
    used = slot_ids < counts[0]
    target = route // capacity
    within = route % capacity
    dest_hot = (
        (target[:, None] == jnp.arange(devices, dtype=jnp.int32)[None, :]) & used[:, None]
    ).astype(jnp.int32)
    earlier = jnp.cumsum(dest_hot, axis=0) - dest_hot
    dest_rank = jnp.sum(earlier * dest_hot, axis=1)
    column = target * pairs + dest_rank
    send_map = (
        (column[:, None] == jnp.arange(lanes, dtype=jnp.int32)[None, :]) & used[:, None]
    ).astype(jnp.bfloat16)
    meta = jnp.stack([within + 1, frame_mask], axis=1).astype(jnp.bfloat16)
    sent_states = jnp.einsum(
        "sl,sd->ld", send_map, start_deter, preferred_element_type=jnp.float32
    ).astype(jnp.bfloat16)
    sent_meta = jnp.einsum("sl,sk->lk", send_map, meta, preferred_element_type=jnp.float32).astype(
        jnp.bfloat16
    )
    got_states, got_meta = (
        lax.all_to_all(sent_states, "dp", split_axis=0, concat_axis=0, tiled=True),
        lax.all_to_all(sent_meta, "dp", split_axis=0, concat_axis=0, tiled=True),
    )
    placing = (
        got_meta[:, 0].astype(jnp.float32)[:, None]
        == (jnp.arange(capacity) + 1).astype(jnp.float32)[None, :]
    ).astype(jnp.bfloat16)
    start_h = jnp.einsum("lc,ld->cd", placing, got_states, preferred_element_type=jnp.float32)
    start_mask = jnp.einsum("lc,l->c", placing, got_meta[:, 1], preferred_element_type=jnp.float32)
    running = jnp.zeros((capacity,), jnp.float32)
    columns = []
    for step_index in range(horizon - 1, -1, -1):
        running = rewards[:, step_index] + discount * running
        columns.insert(0, running)
    returns = jnp.stack(columns, axis=1)
    weight_mask = start_mask[:, None]
    total_sum, square_sum, number = lax.psum(
        (
            jnp.sum(weight_mask * returns),
            jnp.sum(weight_mask * returns * returns),
            horizon * jnp.sum(start_mask),
        ),
        ("dp", "rep"),
    )
    centre = total_sum / number
    spread = jnp.sqrt(square_sum / number - centre * centre + norm_eps)
    advantage = (returns - centre) / spread
    latent_hot = (latent_idx[..., None] == jnp.arange(CLASSES, dtype=jnp.int32)).astype(
        jnp.bfloat16
    )
    latent_hot = latent_hot.reshape(capacity, horizon, STOCH)
    action_hot = (action_idx[..., None] == jnp.arange(ACTIONS, dtype=jnp.int32)).astype(
        jnp.bfloat16
    )
    small_weights = (
        act_embed,
        gru_gain.astype(jnp.float32),
        gru_bias.astype(jnp.float32),
        actor_head,
        critic_head,
    )
    per_micro = capacity // MICRO
    loss_total = jnp.zeros((), jnp.float32)
    small_total = None
    start_parts = []
    full_total = None
    for micro_index in range(MICRO):
        span_lo = micro_index * per_micro
        span_hi = span_lo + per_micro
        gathered = lax.all_gather(weights_flat, "dp", axis=0, tiled=True)
        latent_block = jnp.swapaxes(latent_hot[span_lo:span_hi], 0, 1)
        action_block = jnp.swapaxes(action_hot[span_lo:span_hi], 0, 1)
        adv_block = jnp.swapaxes(advantage[span_lo:span_hi], 0, 1)
        mask_block = jnp.broadcast_to(start_mask[None, span_lo:span_hi], (horizon, per_micro))
        kept, loss_part = forward_micro(
            gathered,
            small_weights,
            start_h[span_lo:span_hi],
            latent_block,
            action_block,
            adv_block,
            mask_block,
        )
        flat_grad, small_grads, start_part = backward_micro(
            gathered, small_weights, kept, latent_block, action_block
        )
        loss_total = loss_total + loss_part
        start_parts.append(start_part)
        if small_total is None:
            small_total = small_grads
        else:
            small_total = tuple((old + new for old, new in zip(small_total, small_grads)))
        full_total = flat_grad if full_total is None else full_total + flat_grad
    weight_part = lax.psum_scatter(full_total, "dp", scatter_dimension=0, tiled=True)
    weight_shard = lax.psum(weight_part.astype(jnp.bfloat16), "rep").astype(jnp.float32)
    summed = lax.psum((loss_total,) + small_total, ("dp", "rep"))
    start_grad = jnp.concatenate(start_parts, 0)
    to_lanes = jnp.dot(placing.astype(jnp.float32), start_grad, precision=lax.Precision.HIGHEST)
    came_back = lax.all_to_all(
        to_lanes.astype(jnp.bfloat16), "dp", split_axis=0, concat_axis=0, tiled=True
    ).astype(to_lanes.dtype)
    frame_grad = jnp.dot(send_map.astype(jnp.float32), came_back, precision=lax.Precision.HIGHEST)
    return (
        summed[0],
        frame_grad,
        weight_shard,
        summed[1],
        summed[2],
        summed[3],
        summed[4],
        summed[5],
    )


def solution(mesh):
    return jax.shard_map(
        on_device,
        mesh=mesh,
        in_specs=(
            P(("dp", "rep"), None),
            P(("dp", "rep")),
            P(("dp", "rep")),
            P(("dp", "rep")),
            P("dp"),
            P(),
            P(),
            P(),
            P(),
            P(),
            P(("dp", "rep"), None, None),
            P(("dp", "rep"), None),
            P(("dp", "rep"), None),
        ),
        out_specs=(P(), P(("dp", "rep"), None), P("dp"), P(), P(), P(), P(), P()),
        check_vma=False,
    )
```

profile of v0, /device:TPU:0, one launch (start us, length us, event | category | flops | bytes accessed | tf_op | source)
XLA Modules:
  0.0 1595.3 jit_solution(8766193378948511434)
XLA Ops:
  11.3 8.4 all-to-all-start
  23.3 5.4 fusion.249
  30.7 4.3 slice.458
  36.1 6.2 fusion.256
  42.3 5.8 slice.448
  53.2 5.2 slice.478
  58.4 4.0 slice.473
  67.5 6.9 all-to-all-start.1
  77.4 45.3 %all-reduce.2 = (f32[]{:T(128)}, f32[]{:T(128)}, f32[]{:T(128)}) all-reduce(f32[]{:T(128)} %get-tuple-element.960, f32[]{:T(128)S(6)} %mul.1011, f32[]{:T(128)} %get-tuple-element.959), channel_id=1, replica_groups=mesh['dp'=16,'rep'=2] {'dp','rep'}, use_global_device_ids=true, to_apply=%region_7.8 | all-reduce | flops 3 | bytes 24 | tf_op jit(solution)/shard_map/psum | solution.py:296
  126.3 3.2 all-gather.2.cloned.1.call-done
  134.5 2.9 fusion.263
  147.1 3.1 slice.512
  150.3 5.6 reshape.620
  159.5 80.8 %while.80 = (s32[]{:T(128)}, f32[24,512]{1,0:T(8,128)S(1)}, f32[15,24,512]{2,1,0:T(8,128)}, f32[15,24,512]{2,1,0:T(8,128)}, f32[15,24,1536]{2,1,0:T(8,128)}, /*i...) while((s32[]{:T(128)}, f32[24,512]{1,0:T(8,128)S(1)}, ...), condition=%wide.region_11.12_spmd, body=%wide.region_8.11_spmd.sunk | while | flops 101658648 | bytes 6100977 | solution.py:114
  257.9 80.9 %while.81 = (s32[]{:T(128)}, f32[24,512]{1,0:T(8,128)S(1)}, f32[15,24,512]{2,1,0:T(8,128)}, f32[15,24,512]{2,1,0:T(8,128)}, f32[15,24,1536]{2,1,0:T(8,128)}, /*i...) while((s32[]{:T(128)}, f32[24,512]{1,0:T(8,128)S(1)}, ...), condition=%wide.region_20.22_spmd, body=%wide.region_17.21_spmd.sunk | while | flops 101658648 | bytes 6100977 | solution.py:114
  355.7 161.3 %while.82 = (s32[]{:T(128)}, f32[24,512]{1,0:T(8,128)S(1)}, bf16[15,24,1536]{2,1,0:T(8,128)(2,1)}, bf16[15,24,512]{2,1,0:T(8,128)(2,1)}, f32[15,1536]{1,0:T(8,12...) while((s32[]{:T(128)}, f32[24,512]{1,0:T(8,128)S(1)}, ...), condition=%wide.region_32.34_spmd, body=%wide.region_25.33_spmd.sunk | while | flops 77730840 | bytes 5763241 | solution.py:209
  517.1 4.1 convolution_bitcast_fusion.2
  521.2 2.8 convolution_bitcast_fusion.3
  537.1 180.3 %while.83 = (s32[]{:T(128)}, f32[24,512]{1,0:T(8,128)S(1)}, bf16[15,24,1536]{2,1,0:T(8,128)(2,1)}, bf16[15,24,512]{2,1,0:T(8,128)(2,1)}, f32[15,1536]{1,0:T(8,12...) while((s32[]{:T(128)}, f32[24,512]{1,0:T(8,128)S(1)}, ...), condition=%wide.region_40.42_spmd, body=%wide.region_33.41_spmd.sunk | while | flops 77730840 | bytes 5763241 | solution.py:209
  717.4 4.2 convolution_bitcast_fusion
  721.6 2.8 convolution_bitcast_fusion.1
  739.7 4.5 all-to-all-start.2
  748.8 3.1 pad_maximum_fusion.2
  751.9 7.3 reshape.625
  769.8 3.0 pad_maximum_fusion.3
  772.8 7.0 reshape.631
  787.3 2.9 constant_dynamic-update-slice_fusion.8
  797.7 2.9 constant_dynamic-update-slice_fusion.9
  806.4 3.0 copy-done.2
  809.4 11.8 add.633
  821.2 720.5 %all-reduce.9 = bf16[4194304]{0:T(1024)(128)(2,1)} all-reduce(f32[4194304]{0:T(1024)} %add.633), channel_id=2, replica_groups=mesh['dp'=16,'rep'=2] {'dp'}, use_global_device_ids=true, to_apply=%region_41.43.clone | all-reduce | flops 4194304 | bytes 25165824
  1546.0 38.8 %all-reduce.8 = (f32[]{:T(128)}, f32[18,512]{1,0:T(8,128)}, f32[1536]{0:T(1024)}, f32[1536]{0:T(1024)}, f32[512,18]{0,1:T(8,128)}, /*index=5*/f32[512]{0:T(512)}) all-reduce(f32[]{:T(128)S(6)} %add.624, f32[18,512]{1,0:T(8,128)S(1)} %fusion.140, f32[1536]{0:T(1024)S(1)} %add.635, ...), channel_id=1, replica_groups=mesh['dp'=16,'rep'=2] {'dp','rep'}, use_global_device_ids=true, to_apply=%region_24.26 | all-reduce | flops 22017 | bytes 176136 | tf_op jit(solution)/shard_map/psum | solution.py:355
  (1180 shorter events, 645.3 us)
Async XLA Ops:
  7.2 27.8 %copy-start = (bf16[96,512]{1,0:T(8,128)(2,1)S(1)}, bf16[96,512]{1,0:T(8,128)(2,1)}, u32[]{:S(2)}) copy-start(bf16[96,512]{1,0:T(8,128)(2,1)} %param.22) | copy-start | bytes 294916
  7.2 122.3 %all-gather.2.cloned.1.call-start = ((), (), s32[]{:S(2)}) async-start(), calls=%async_computation.3 | async-start | bytes 8912896 | tf_op jit(solution)/shard_map/all_gather | solution.py:329
  8.6 26.4 %copy-start.93 = (pred[96]{0:T(512)(128)(4,1)}, pred[96]{0:T(512)(128)(4,1)S(1)}, u32[]{:S(2)}) copy-start(pred[96]{0:T(512)(128)(4,1)S(1)} %iota_compare_fusion.4) | copy-start | bytes 292
  10.3 24.6 %copy-start.98 = (s32[96]{0:T(128)}, s32[96]{0:T(128)S(1)}, u32[]{:S(2)}) copy-start(s32[96]{0:T(128)S(1)} %multiply_add_fusion.19) | copy-start | bytes 1156
  11.3 56.3 %all-to-all-start = ((bf16[16,12,2]{1,2,0:T(2,128)(2,1)}), bf16[16,12,2]{1,2,0:T(2,128)(2,1)}, u32[]{:S(2)}, u32[]{:S(2)}) async-start(bf16[16,12,2]{1,2,0:T(2,128)(2,1)} %copy.38), calls=%async_computation | async-start | bytes 16384 | tf_op jit(solution)/shard_map/all_to_all | solution.py:281
  42.3 7.9 copy-start.96
  42.3 9.5 copy-start.97
  58.4 6.9 copy-start.86
  58.4 7.8 copy-start.102
  67.5 58.4 %all-to-all-start.1 = ((bf16[16,12,512]{2,1,0:T(8,128)(2,1)}), bf16[16,12,512]{2,1,0:T(8,128)(2,1)S(1)}, u32[]{:S(2)}, u32[]{:S(2)}) async-start(bf16[16,12,512]{2,1,0:T(8,128)(2,1)} %all_to_all.27), calls=%async_computation.1 | async-start | bytes 524288 | tf_op jit(solution)/shard_map/all_to_all | solution.py:280
  343.7 8.0 copy-start.42
  344.5 7.1 copy-start.70
  736.9 7.4 copy-start.34
  736.9 7.4 copy-start.56
  739.7 845.2 %all-to-all-start.2 = ((bf16[16,12,512]{2,1,0:T(8,128)(2,1)}), bf16[16,12,512]{2,1,0:T(8,128)(2,1)S(1)}, u32[]{:S(2)}, u32[]{:S(2)}) async-start(bf16[16,12,512]{2,1,0:T(8,128)(2,1)} %all_to_all.30), calls=%async_computation.2 | async-start | bytes 524288 | tf_op jit(solution)/shard_map/all_to_all | solution.py:358
  744.2 841.6 %all-reduce.7.cloned.1.call-start = ((), (), s32[]{:S(2)}) async-start(), calls=%async_computation.4 | async-start | bytes 1048576 | tf_op jit(solution)/shard_map/psum | solution.py:354
  751.9 7.3 copy-start.12
  751.9 7.3 copy-start.22
  790.2 7.6 slice-start.2
  800.6 8.8 copy-start.2
  821.2 722.5 %copy-start.57 = (bf16[15,24,512]{2,1,0:T(8,128)(2,1)S(1)}, bf16[15,24,512]{2,1,0:T(8,128)(2,1)}, u32[]{:S(2)}) copy-start(bf16[15,24,512]{2,1,0:T(8,128)(2,1)} %get-tuple-element.843) | copy-start | bytes 1105924
  821.2 722.5 %copy-start.87 = (pred[16,24,18]{1,0,2:T(8,128)(4,1)S(1)}, pred[16,24,18]{1,0,2:T(8,128)(4,1)}, u32[]{:S(2)}) copy-start(pred[16,24,18]{1,0,2:T(8,128)(4,1)} %get-tuple-element.1126) | copy-start | bytes 20740
  821.2 722.5 %copy-start.88 = (f32[18,512]{1,0:T(8,128)S(1)}, f32[18,512]{1,0:T(8,128)}, u32[]{:S(2)}) copy-start(f32[18,512]{1,0:T(8,128)} %convolution_bitcast_fusion.10) | copy-start | bytes 110596
  821.2 722.8 %copy-start.54 = (bf16[384,512]{1,0:T(8,128)(2,1)S(1)}, bf16[384,512]{1,0:T(8,128)(2,1)}, u32[]{:S(2)}) copy-start(bf16[384,512]{1,0:T(8,128)(2,1)} %copy-done.53) | copy-start | bytes 1179652
  821.2 724.3 %copy-start.78 = (f32[15,1536]{1,0:T(8,128)S(1)}, f32[15,1536]{1,0:T(8,128)}, u32[]{:S(2)}) copy-start(f32[15,1536]{1,0:T(8,128)} %copy-done.77) | copy-start | bytes 276484
  821.2 724.3 %copy-start.76 = (f32[15,1536]{1,0:T(8,128)S(1)}, f32[15,1536]{1,0:T(8,128)}, u32[]{:S(2)}) copy-start(f32[15,1536]{1,0:T(8,128)} %copy-done.75) | copy-start | bytes 276484
  821.2 724.4 %copy-start.79 = (f32[15,1536]{1,0:T(8,128)S(1)}, f32[15,1536]{1,0:T(8,128)}, u32[]{:S(2)}) copy-start(f32[15,1536]{1,0:T(8,128)} %get-tuple-element.850) | copy-start | bytes 276484
  821.2 724.4 %copy-start.67 = (f32[384,512]{1,0:T(8,128)S(1)}, f32[384,512]{1,0:T(8,128)}, u32[]{:S(2)}) copy-start(f32[384,512]{1,0:T(8,128)} %copy-done.66) | copy-start | bytes 2359300
  821.2 724.4 %copy-start.92 = (bf16[384,18]{0,1:T(8,128)(2,1)S(1)}, bf16[384,18]{0,1:T(8,128)(2,1)}, u32[]{:S(2)}) copy-start(bf16[384,18]{0,1:T(8,128)(2,1)} %copy-done.91) | copy-start | bytes 41476
  1541.7 43.2 %copy-start.94 = (pred[96]{0:T(512)(128)(4,1)S(1)}, pred[96]{0:T(512)(128)(4,1)}, u32[]{:S(2)}) copy-start(pred[96]{0:T(512)(128)(4,1)} %copy-done.93) | copy-start | bytes 292
  1541.7 43.2 %copy-start.99 = (s32[96]{0:T(128)S(1)}, s32[96]{0:T(128)}, u32[]{:S(2)}) copy-start(s32[96]{0:T(128)} %copy-done.98) | copy-start | bytes 1156
  1541.7 46.2 %copy-start.1 = (bf16[96,512]{1,0:T(8,128)(2,1)S(1)}, bf16[96,512]{1,0:T(8,128)(2,1)}, u32[]{:S(2)}) copy-start(bf16[96,512]{1,0:T(8,128)(2,1)} %param.22) | copy-start | bytes 294916
  (82 other events, 252.9 us)
Sparse Core Ops, SparseCore 0:
  10.8 118.6 all-gather.1
  1543.8 15.2 all-reduce.6
where the time goes:
time: 1610 us; the launch traced here: 1600 us
  blocking collectives  805 us (50%)
  matrix products  280 us (17%)
  other arithmetic  255 us (16%)
  local copies, waits for them, and re-layouts  207 us (13%)
  between operations  21.9 us (1%)
  starting transfers between devices  19.9 us (1%)
    unnamed x1, blocking collectives  721 us
    dot_general x138, matrix products, product(): return jnp.dot(left, right, preferred_element_type=jnp.float32)  128 us
    dot_general x70, matrix products, product_nt(): lax.dot_general(left, right, (((1,), (1,)), ((), ())), preferred_element_...  110 us
    dynamic_update_slice x30, other arithmetic, backward_micro(): lax.scan(back_step, state_grad[-1], (states, pre_acts, gru_raws, state_gr...  49.5 us
    unnamed x240, local copies, waits for them, and re-layouts  45.8 us
    psum x1, blocking collectives, on_device(): lax.psum((jnp.sum(weight_mask * returns), jnp.sum(weight_mask * returns *...  45.3 us
    reduce_sum x60, other arithmetic, gru_update(): jnp.mean(centred * centred, axis=-1, keepdims=True) + norm_eps  39.3 us
    dot_general x22, matrix products, product_t(): lax.dot_general(left, right, (((0,), (0,)), ((), ())), preferred_element_...  39.2 us
  transfers between devices with their start and end apart: 5, of which 1 were waited for; matrix products, arithmetic and copies ran while one was open for 8% of the time, Pallas kernels for 0%

commit v1 on v0

v1 whole, which is shorter than its diff:
```python
import functools
from types import SimpleNamespace

import jax
import jax.numpy as jnp
from jax import lax
from jax.experimental import pallas as pl
from jax.experimental.pallas import tpu as pltpu
from jax.sharding import PartitionSpec as P

DET = 512
CLASSES = 32
LATENTS = 32
ACTIONS = 18
STOCH = 1024
GATES = 1536
WIDE = 256
META = 128
BLOCK = 192
TALL = 384
LAG_A, LAG_B, LAG_Z = 2, 4, 1

discount = 0.99
entropy_weight = 0.1
norm_eps = 1e-05

F32 = jnp.float32
BF16 = jnp.bfloat16
MESH = pl.DeviceIdType.MESH

ROW_WIN, ROW_GRU, ROW_A1, ROW_A2, ROW_C1, ROW_C2 = 0, 1024, 4096, 5632, 6144, 7680
SM_EMBED, SM_GAIN, SM_BIAS, SM_ACTOR, SM_CRITIC, SM_LOSS = 0, 48, 54, 64, 112, 114


def dot(left, right):
    return jnp.dot(left, right, preferred_element_type=F32)


def dot_t(left, right):
    return lax.dot_general(left, right, (((0,), (0,)), ((), ())), preferred_element_type=F32)


def dot_nt(left, right):
    return lax.dot_general(left, right, (((1,), (1,)), ((), ())), preferred_element_type=F32)


def elu(value):
    near = value + 0.5 * value * value
    below = jnp.where(value > -0.00390625, near, jnp.exp(jnp.minimum(value, 0.0)) - 1.0)
    return jnp.where(value > 0, value, below)


def elu_grad(value):
    return jnp.where(value > 0, 1.0, jnp.exp(jnp.minimum(value, 0.0)))


def iota(shape, dim):
    return lax.broadcasted_iota(jnp.int32, shape, dim)


def mult(value, step):
    return pl.multiple_of(value, step)


class Plan:
    def __init__(self, devices, slots, cap, horizon, flat_rows):
        self.n = devices
        self.line = devices // 4
        self.half = self.line // 2
        self.rows = flat_rows // devices
        self.slots = slots
        self.cap = cap
        self.horizon = horizon
        self.all_rows = cap * horizon
        self.step_rows = cap * (horizon - 1)
        self.lane = -(-max(2, 2 * slots // devices) // 16) * 16
        self.parts = max(1, min(4, self.rows // 2 // 32))
        self.part_rows = self.rows // 2 // self.parts
        self.items = self.half * self.parts
        self.bits = self.line.bit_length() - 1
        self.small = 8 * devices


def kernel_body(plan, names, *refs):
    r = SimpleNamespace(**dict(zip(names, refs)))
    n, line, half, rows = plan.n, plan.line, plan.half, plan.rows
    cap, horizon, parts, prow = plan.cap, plan.horizon, plan.parts, plan.part_rows
    total, steps_rows, lane = plan.all_rows, plan.step_rows, plan.lane
    items, bits = plan.items, plan.bits
    me = lax.axis_index("dp")
    core = lax.axis_index("rep")
    z = me // 4
    a_step = 1 + core
    b_step = 2 - core
    a_bit = (me // a_step) % 2
    b_bit = (me // b_step) % 2
    a_dev = me + a_step * (1 - 2 * a_bit)
    b_dev = me + b_step * (1 - 2 * b_bit)
    q = me % 4
    q_a = a_dev % 4
    q_b = b_dev % 4
    q_ab = 3 - q
    sibling = 1 - core

    def remote(src, dst, send, recv, dev, on_core=None):
        return pltpu.make_async_remote_copy(
            src_ref=src,
            dst_ref=dst,
            send_sem=send,
            recv_sem=recv,
            device_id=(dev, core if on_core is None else on_core),
            device_id_type=MESH,
        )

    barrier = pltpu.get_barrier_semaphore()

    def greet(k, carry):
        pl.semaphore_signal(barrier, inc=1, device_id=((me + k) % n, core), device_id_type=MESH)
        return carry

    lax.fori_loop(1, n, greet, 0)
    pl.semaphore_signal(barrier, inc=1, device_id=(me, sibling), device_id_type=MESH)

    full = r.full
    own_rows = pl.ds(mult(me * rows + core * (rows // 2), 16), rows // 2)
    r.narrow[...] = r.weights[pl.ds(mult(core * rows * 2, 16), rows * 2)].astype(F32)
    for c in range(4):
        full[own_rows, 128 * c : 128 * (c + 1)] = r.narrow[pl.ds(c, rows // 2, stride=4), :].astype(BF16)

    route = r.route[...].astype(F32)
    slots = plan.slots
    used_row = (iota((1, slots), 1) < r.counts[...]).astype(F32)
    target_row = jnp.floor((route + 0.5) * (1.0 / cap))
    within_row = route - cap * target_row
    eye = iota((slots, slots), 0) == iota((slots, slots), 1)
    target_col = jnp.sum(jnp.where(eye, target_row, 0.0), axis=1, keepdims=True)
    used_col = jnp.sum(jnp.where(eye, used_row, 0.0), axis=1, keepdims=True)
    earlier = iota((slots, slots), 0) < iota((slots, slots), 1)
    same = jnp.where(earlier & (target_col == target_row), used_col, 0.0)
    rank_row = jnp.sum(same, axis=0, keepdims=True)
    column_row = jnp.where(used_row > 0, target_row * lane + rank_row, -1.0)
    lanes = n * lane
    tall = min(lanes, 256)

    def each(low, high, body):
        def step(k, carry):
            body(k)
            return carry

        lax.fori_loop(low, high, step, 0)

    def to_lanes(k):
        block = pl.ds(mult(k * tall, 16), tall)
        chosen_slot = column_row == (iota((tall, slots), 0) + k * tall).astype(F32)
        picked = jnp.where(chosen_slot, 1.0, 0.0).astype(BF16)
        r.to_lane[block] = picked
        place = jnp.sum(jnp.where(chosen_slot, within_row + 1.0, 0.0), axis=1, keepdims=True)
        marked = jnp.sum(
            jnp.where(chosen_slot, r.frame_mask[...].astype(F32), 0.0), axis=1, keepdims=True
        )
        meta_lane = iota((tall, META), 1)
        meta = jnp.where(meta_lane == 0, place, jnp.where(meta_lane == 1, marked, 0.0))
        r.sent[block, :DET] = dot(picked, r.start_deter[...]).astype(BF16)
        r.sent[block, DET:] = meta.astype(BF16)

    each(0, lanes // tall, to_lanes)

    pl.semaphore_wait(barrier, n)

    def lane_rows(k):
        return pl.ds(mult(k * lane, 16), lane)

    def exchange(width, sends, recvs):
        src, dst = r.sent, r.got

        def copy(k, to, into):
            return remote(
                src.at[lane_rows(to), 0:width], dst.at[lane_rows(into), 0:width], sends.at[k], recvs.at[k], to
            )

        def begin():
            dst[lane_rows(me), 0:width] = src[lane_rows(me), 0:width]
            each(1, n, lambda k: copy(k, (me + k) % n, me).start())

        def finish():
            each(1, n, lambda k: copy(k, me, (me + n - k) % n).wait_recv())

        def drain():
            each(1, n, lambda k: copy(k, (me + k) % n, me).wait_send())

        return begin, finish, drain

    out_begin, out_finish, out_drain = exchange(DET + META, r.ex_send, r.ex_recv)
    def bit_of(value, b):
        return (value // 2**b) % 2

    def across(b):
        return me + 4 * 2**b * (1 - 2 * bit_of(z, b))

    def item_at(i):
        group = i // items
        inner = i % items
        order = inner // parts
        place = z % half
        for b in range(bits - 1):
            place = place + bit_of(order, b) * 2**b * (1 - 2 * bit_of(z, b))
        return group, order, group * half + place, inner % parts

    def full_at(shard, piece, part):
        return full.at[pl.ds(mult(shard * rows + part * (rows // 2) + piece * prow, 16), prow)]

    def gather_copy(shard, piece, send, dev):
        view = full_at(shard, piece, core)
        return remote(view, view, send, r.ag_recv.at[shard, piece], dev)

    def share_copy(shard, piece, send, part=None):
        view = full_at(shard, piece, core if part is None else part)
        return remote(view, view, send, r.sh_recv.at[shard, piece], me, sibling)

    def far_copy(piece):
        return gather_copy(me, piece, r.far_send.at[piece], across(bits - 1))

    def plane_sends(zi, piece):
        mine = zi * 4 + q
        other = zi * 4 + q_a
        return (
            gather_copy(mine, piece, r.a_send.at[zi, piece], a_dev),
            gather_copy(mine, piece, r.b_send.at[zi, piece, 0], b_dev),
            gather_copy(other, piece, r.b_send.at[zi, piece, 1], b_dev),
        )

    def line_sends(order, zi, piece):
        return [
            (order < 2**b, gather_copy(zi * 4 + q, piece, r.line_send.at[zi, piece, b], across(b)))
            for b in range(bits - 1)
        ]

    def gather_line(i):
        _, order, zi, piece = item_at(i)

        @pl.when(zi != z)
        def _():
            gather_copy(zi * 4 + q, piece, r.a_send.at[zi, piece], me).wait_recv()

        for need, copy in line_sends(order, zi, piece):
            pl.when(need)(copy.start)
        to_a, to_b, _ = plane_sends(zi, piece)
        to_a.start()
        to_b.start()
        share_copy(zi * 4 + q, piece, r.sh_send.at[zi, piece, 0]).start()

    def gather_a(i):
        _, _, zi, piece = item_at(i)
        gather_copy(zi * 4 + q_a, piece, r.a_send.at[zi, piece], me).wait_recv()
        plane_sends(zi, piece)[2].start()
        share_copy(zi * 4 + q_a, piece, r.sh_send.at[zi, piece, 1]).start()

    def gather_b(i):
        _, _, zi, piece = item_at(i)
        for k, where in ((2, q_b), (3, q_ab)):
            gather_copy(zi * 4 + where, piece, r.a_send.at[zi, piece], me).wait_recv()
            share_copy(zi * 4 + where, piece, r.sh_send.at[zi, piece, k]).start()

    def gather_shared(i):
        _, _, zi, piece = item_at(i)
        for k, where in ((0, q), (1, q_a), (2, q_b), (3, q_ab)):
            share_copy(zi * 4 + where, piece, r.sh_send.at[zi, piece, k], sibling).wait_recv()

    def gather_drain(i):
        _, order, zi, piece = item_at(i)
        for need, copy in line_sends(order, zi, piece):
            pl.when(need)(copy.wait_send)
        for copy in plane_sends(zi, piece):
            copy.wait_send()
        for k, where in ((0, q), (1, q_a), (2, q_b), (3, q_ab)):
            share_copy(zi * 4 + where, piece, r.sh_send.at[zi, piece, k]).wait_send()

    lag_a, lag_b = LAG_A, LAG_B
    all_items = 2 * items
    ticks = all_items + lag_b
    first_ticks = items + lag_b

    def gather_tick(k):
        pl.when(k < all_items)(lambda: gather_line(k))
        pl.when((k >= lag_a) & (k < all_items + lag_a))(lambda: gather_a(k - lag_a))
        pl.when((k >= lag_b) & (k < all_items + lag_b))(lambda: gather_b(k - lag_b))

    each(0, parts, lambda piece: far_copy(piece).start())
    early = min(2, first_ticks)
    each(0, early, gather_tick)
    out_begin()

    hot, hot_t, act_hot = r.hot, r.hot_t, r.act_hot
    for t in range(horizon):
        r.latent_row[:, t * cap : (t + 1) * cap] = r.latent[t].astype(F32)
        r.action_row[:, t * cap : (t + 1) * cap] = r.action[t : t + 1].astype(F32)
    latent_row = r.latent_row[...].astype(BF16)
    spread_rows = (iota((LATENTS, STOCH), 1) // CLASSES == iota((LATENTS, STOCH), 0)).astype(F32).astype(BF16)
    class_row = (iota((1, STOCH), 1) % CLASSES).astype(F32)
    latent_col = latent_row.T
    for k in range(total // 128):
        seen = dot(latent_col[128 * k : 128 * (k + 1)], spread_rows)
        hot[128 * k : 128 * (k + 1)] = jnp.where(seen == class_row, 1.0, 0.0).astype(BF16)

    def hot_t_block(k):
        block = pl.ds(mult(k * 128, 128), 128)
        first = k * 128
        spread = ((iota((128, LATENTS), 0) + first) // CLASSES == iota((128, LATENTS), 1)).astype(F32).astype(BF16)
        seen = dot(spread, latent_row)
        class_col = ((iota((128, 1), 0) + first) % CLASSES).astype(F32)
        hot_t[block] = jnp.where(seen == class_col, 1.0, 0.0).astype(BF16)

    each(0, STOCH // 128, hot_t_block)
    act_hot[...] = jnp.where(r.action_row[...] == iota((128, total), 0).astype(F32), 1.0, 0.0).T.astype(BF16)

    r.embed_pad[...] = jnp.zeros((32, DET), BF16)
    r.embed_pad[0:ACTIONS] = r.act_embed[...]
    r.head_pad[...] = jnp.zeros((128, DET), BF16)
    r.head_pad[0:ACTIONS] = r.actor_head[...]
    r.small[...] = jnp.zeros(r.small.shape, F32)

    each(early, first_ticks, gather_tick)

    out_finish()
    r.start[...] = jnp.zeros((128, DET + META), F32)

    def from_lanes(k):
        block = pl.ds(mult(k * tall, 16), tall)
        got = r.got[block]
        put = jnp.where(got[:, DET : DET + 1].astype(F32) == (iota((tall, 128), 1) + 1).astype(F32), 1.0, 0.0).astype(BF16)
        r.placing[block] = put
        r.start[...] += dot_t(put, got)

    each(0, lanes // tall, from_lanes)
    start = r.start
    states_ref = r.states
    states_ref[0:cap] = start[0:cap, 0:DET]
    mask = start[0:cap, DET + 1 : DET + 2]
    eye = iota((cap, cap), 0) == iota((cap, cap), 1)
    mask_row = jnp.sum(jnp.where(eye, mask, 0.0), axis=0, keepdims=True)
    adv = r.adv
    running = jnp.zeros((1, cap), F32)
    sum_one = jnp.zeros((1, cap), F32)
    sum_two = jnp.zeros((1, cap), F32)
    for t in range(horizon - 1, -1, -1):
        running = r.rewards[t : t + 1] + discount * running
        sum_one = sum_one + mask_row * running
        sum_two = sum_two + mask_row * running * running
        r.returns[:, t * cap : (t + 1) * cap] = running
        r.weight_row[:, t * cap : (t + 1) * cap] = mask_row * (1.0 / horizon)
    tile_lane = iota((8, 128), 1)

    def total_of(value):
        return jnp.sum(value, axis=1, keepdims=True)

    sums = jnp.where(
        tile_lane == 0,
        total_of(sum_one),
        jnp.where(tile_lane == 1, total_of(sum_two), jnp.where(tile_lane == 2, horizon * total_of(mask_row), 0.0)),
    )
    moments, pair = r.moments, r.pair
    pair[0] = sums
    swap = remote(pair.at[0], pair.at[1], r.pair_sem.at[0], r.pair_sem.at[1], me, sibling)
    swap.start()
    each(0, items, gather_shared)
    swap.wait()
    moments[me] = pair[0] + pair[1]

    def moments_copy(k):
        peer = (me + k) % n
        return remote(moments.at[me], moments.at[me], r.mo_send.at[k], r.mo_recv.at[k], peer)

    def moments_landing(k):
        peer = (me + n - k) % n
        return remote(moments.at[peer], moments.at[peer], r.mo_send.at[k], r.mo_recv.at[k], peer)

    each(1, n, lambda k: moments_copy(k).start())

    shuffle = r.shuffle
    row_i = iota((TALL, TALL), 0)
    shuffle[...] = jnp.where(
        iota((TALL, TALL), 1) == 3 * (row_i % 128) + row_i // 128, 1.0, 0.0
    ).astype(BF16)
    w_gru = r.w_gru
    for j in range(8):
        block = full[ROW_GRU + TALL * j : ROW_GRU + TALL * (j + 1)]
        sorted_rows = dot(shuffle[...], block).astype(BF16)
        for k in range(3):
            w_gru[128 * j : 128 * (j + 1), DET * k : DET * (k + 1)] = sorted_rows[128 * k : 128 * (k + 1)]
    each(0, items, gather_drain)
    each(0, parts, lambda piece: pl.when(z < half)(far_copy(piece).wait_send))
    w_back = full.at[ROW_GRU : ROW_GRU + GATES]
    for j in range(4):
        for k in range(3):
            w_back[DET * k : DET * (k + 1), 128 * j : 128 * (j + 1)] = w_gru[
                DET + 128 * j : DET + 128 * (j + 1), DET * k : DET * (k + 1)
            ].T

    pre, inputs, raw = r.pre, r.inputs, r.raw
    low, work = r.low, r.work
    a_one_at, a_two_at, g_one, g_two = 0, 2 * DET, 4 * DET, 6 * DET
    p_low = GATES
    inputs[steps_rows:total] = jnp.zeros((total - steps_rows, DET), BF16)
    pre_block = 5 * cap

    def pre_step(k):
        block = pl.ds(mult(k * pre_block, 16), pre_block)
        value = dot(hot[block], full[ROW_WIN : ROW_WIN + STOCH])
        value = value + dot(act_hot[block][:, 0:32], r.embed_pad[...])
        pre[block] = value
        active = elu(value).astype(BF16)
        inputs[block] = active
        raw[block] = dot(active, w_gru[0:DET])
        gather_tick(first_ticks + k)

    pre_blocks = (horizon - 1) // 5
    each(0, pre_blocks, pre_step)

    def as_row(ref):
        value = ref[...].astype(F32)
        return jnp.concatenate([value[k : k + 1] for k in range(ref.shape[0])], axis=-1)

    gain = as_row(r.gain)
    bias = as_row(r.bias)
    update_ref, inv_ref = r.update, r.inv

    def forward_step(t):
        block = pl.ds(mult(t * cap, 16), cap)
        state = states_ref[block]
        state_low = state.astype(BF16)
        low[block] = state_low
        gru_raw = raw[block] + dot(state_low, w_gru[DET:])
        centred = gru_raw - jnp.mean(gru_raw, axis=-1, keepdims=True)
        inv_std = lax.rsqrt(jnp.mean(centred * centred, axis=-1, keepdims=True) + norm_eps)
        normed = centred * inv_std
        raw[block] = normed
        inv_ref[block] = jnp.broadcast_to(inv_std, (cap, 128))
        mixed = normed * gain + bias
        reset = jax.nn.sigmoid(mixed[:, :DET])
        candidate = jnp.tanh(reset * mixed[:, DET : 2 * DET])
        update = jax.nn.sigmoid(mixed[:, 2 * DET :] - 1.0)
        update_ref[block] = update
        states_ref[pl.ds(mult(t * cap + cap, 16), cap)] = update * candidate + (1.0 - update) * state
        pl.when(t % 3 == 2)(lambda: gather_tick(first_ticks + pre_blocks + t // 3))

    each(0, horizon - 1, forward_step)
    done_ticks = first_ticks + pre_blocks + (horizon - 1) // 3
    each(done_ticks, max(ticks, done_ticks), gather_tick)
    low[steps_rows:total] = states_ref[steps_rows:total].astype(BF16)
    each(items, 2 * items, gather_shared)
    each(items, 2 * items, gather_drain)
    each(0, parts, lambda piece: pl.when(z >= half)(far_copy(piece).wait_send))

    each(1, n, lambda k: moments_landing(k).wait_recv())
    sums = moments[0]
    for k in range(1, n):
        sums = sums + moments[k]
    centre = sums[0:1, 0:1] / sums[0:1, 2:3]
    spread = jnp.sqrt(sums[0:1, 1:2] / sums[0:1, 2:3] - centre * centre + norm_eps)
    per_row = jnp.concatenate(
        [(r.returns[...] - centre) / spread, r.weight_row[...], jnp.zeros((126, total), F32)], axis=0
    ).T
    adv[...] = per_row

    grads = r.grads

    def keep_grads(first, value):
        for c in range(4):
            grads[c, pl.ds(first, value.shape[0])] = value[:, 128 * c : 128 * (c + 1)]

    def load_grads(block):
        return jnp.concatenate([grads[c, block] for c in range(4)], axis=-1)

    def grad_rows(local, part, piece):
        return pl.ds(mult(local * rows + part * (rows // 2) + piece * prow, 16), prow)

    def store_grads(block, value):
        for c in range(4):
            grads[c, block] = value[:, 128 * c : 128 * (c + 1)]

    pair_in, b_in, a_in, z_in = r.pair_in, r.b_in, r.a_in, r.z_in

    class Reducer:
        def __init__(self, group):
            self.group = group
            self.turn = half // 2 if group == 0 else 0

        def target(self, i):
            return (i // parts + self.turn) % half, i % parts

        def sem(self, array, *at):
            return array.at[(self.group,) + at]

        def out_rows(self, t, offset, piece, count):
            return pl.ds(mult(ROW_A1 + t * 4 * rows + offset + piece * count * prow, 16), count * prow)

        def in_rows(self, t, piece, count):
            return pl.ds(mult((t * parts + piece) * count * prow, 16), count * prow)

        def pair_copy(self, t, piece):
            return remote(
                full.at[self.out_rows(t, 0, piece, 4)],
                pair_in.at[self.in_rows(t, piece, 4)],
                self.sem(r.pair_s, t, piece),
                self.sem(r.pair_r, t, piece),
                me,
                sibling,
            )

        def b_copy(self, t, piece):
            return remote(
                full.at[self.out_rows(t, 2 * rows, piece, 2)],
                b_in.at[self.group, self.in_rows(t, piece, 2)],
                self.sem(r.b_s, t, piece),
                self.sem(r.b_r, t, piece),
                b_dev,
            )

        def a_copy(self, t, piece):
            return remote(
                full.at[self.out_rows(t, 3 * rows, piece, 1)],
                a_in.at[self.group, self.in_rows(t, piece, 1)],
                self.sem(r.a_s, t, piece),
                self.sem(r.a_r, t, piece),
                a_dev,
            )

        def z_slot(self, b, t):
            return sum(half // 2 ** (k + 1) for k in range(b)) + t // 2 ** (b + 1)

        def z_copy(self, b, t, piece):
            slot = self.z_slot(b, t)
            return remote(
                full.at[self.out_rows(t, 3 * rows + rows // 2, piece, 1)],
                z_in.at[self.group, self.in_rows(slot, piece, 1)],
                self.sem(r.z_s, t, piece),
                self.sem(r.z_r, slot, piece),
                across(b),
            )

        def holds(self, b, t):
            return (z - t - self.group * half) % 2**b == 0

        def differs(self, b, t):
            return bit_of(z, b) != bit_of(t + self.group * half, b)

        def fin_rows(self, piece, part):
            return pl.ds(mult((part * (rows // 2) + piece * prow) * 4, 16), prow * 4)

        def fin_copy(self, piece, part=None):
            block = self.fin_rows(piece, core if part is None else part)
            return remote(
                r.weights_grad.at[block], r.weights_grad.at[block], r.fin_s.at[piece], r.fin_r.at[piece], me, sibling
            )

        def load(self, t, piece, a):
            if self.group == 0:
                return load_grads(grad_rows(t * 4 + a * a_step + b_bit * b_step, core, piece))
            return r.kept[(t * parts + piece) * 2 + a]

        def store(self, t, piece, a, value):
            if self.group == 0:
                store_grads(grad_rows(t * 4 + a * a_step + b_bit * b_step, core, piece), value)
            else:
                r.kept[(t * parts + piece) * 2 + a] = value

        def to_pair(self, i):
            t, piece = self.target(i)
            for k in range(4):
                block = pl.ds(mult(ROW_A1 + t * 4 * rows + (piece * 4 + k) * prow, 16), prow)
                full[block] = load_grads(grad_rows(t * 4 + k, sibling, piece)).astype(BF16)
            self.pair_copy(t, piece).start()

        def to_b(self, i):
            t, piece = self.target(i)
            self.pair_copy(t, piece).wait_recv()

            def both_cores(where):
                spot = pl.ds(mult(((t * parts + piece) * 4 + where) * prow, 16), prow)
                return load_grads(grad_rows(t * 4 + where, core, piece)) + pair_in[spot].astype(F32)

            for a in range(2):
                block = pl.ds(mult(ROW_A1 + t * 4 * rows + 2 * rows + (piece * 2 + a) * prow, 16), prow)
                full[block] = both_cores(a * a_step + (1 - b_bit) * b_step).astype(BF16)
            self.b_copy(t, piece).start()
            for a in range(2):
                self.store(t, piece, a, both_cores(a * a_step + b_bit * b_step))

        def b_part(self, t, piece, a):
            spot = pl.ds(mult(((t * parts + piece) * 2 + a) * prow, 16), prow)
            return b_in[self.group, spot].astype(F32)

        def to_a(self, i):
            t, piece = self.target(i)
            self.b_copy(t, piece).wait_recv()
            other = 1 - a_bit
            full[self.out_rows(t, 3 * rows, piece, 1)] = (
                self.load(t, piece, other) + self.b_part(t, piece, other)
            ).astype(BF16)
            self.a_copy(t, piece).start()
            self.store(t, piece, a_bit, self.load(t, piece, a_bit) + self.b_part(t, piece, a_bit))

        def to_plane(self, b, i):
            t, piece = self.target(i)

            @pl.when(self.holds(b, t))
            def _():
                if b == 0:
                    self.a_copy(t, piece).wait_recv()
                    came = a_in[self.group, self.in_rows(t, piece, 1)]
                else:
                    self.z_copy(b - 1, t, piece).wait_recv()
                    came = z_in[self.group, self.in_rows(self.z_slot(b - 1, t), piece, 1)]
                value = self.load(t, piece, a_bit) + came.astype(F32)
                if b == bits:
                    first = mult((core * (rows // 2) + piece * prow) * 4, 16)
                    for c in range(4):
                        r.weights_grad[pl.ds(first + c, prow, stride=4), :] = value[:, 128 * c : 128 * (c + 1)]
                    self.fin_copy(piece).start()
                else:

                    @pl.when(self.differs(b, t))
                    def _():
                        full[self.out_rows(t, 3 * rows + rows // 2, piece, 1)] = value.astype(BF16)
                        self.z_copy(b, t, piece).start()

                    pl.when(~self.differs(b, t))(lambda: self.store(t, piece, a_bit, value))

        def drain_early(self, i):
            t, piece = self.target(i)
            self.pair_copy(t, piece).wait_send()
            self.b_copy(t, piece).wait_send()

        def drain(self, i):
            t, piece = self.target(i)
            self.a_copy(t, piece).wait_send()
            for b in range(bits):
                pl.when(self.holds(b, t) & self.differs(b, t))(self.z_copy(b, t, piece).wait_send)

            @pl.when(self.holds(bits, t))
            def _():
                self.fin_copy(piece).wait_send()
                self.fin_copy(piece, sibling).wait_recv()

        def tick(self, k):
            pl.when((k >= 0) & (k < items))(lambda: self.to_a(k))
            for b in range(bits + 1):
                j = k - LAG_Z * (b + 1)
                pl.when((j >= 0) & (j < items))(lambda b=b, j=j: self.to_plane(b, j))

    rs_ticks = items + LAG_Z * (bits + 1)
    heads_rs, gru_rs = Reducer(1), Reducer(0)
    net_items = items // 2

    out_grads, state_grads = r.out_grads, r.state_grads
    r.loss_acc[...] = jnp.zeros((BLOCK, 128), F32)
    critic_row = as_row(r.critic_head)
    lane_id = iota((BLOCK, 128), 1)

    def net_rows(side):
        return (ROW_A1, ROW_A2) if side == 0 else (ROW_C1, ROW_C2)

    def net_cols(base, side):
        return slice(base + side * DET, base + (side + 1) * DET)

    def net_step(k, side):
        first, second = net_rows(side)
        block = pl.ds(mult(k * BLOCK, 64), BLOCK)
        one = dot(low[block], full[first : first + DET]) + dot(hot[block], full[first + DET : first + DET + STOCH])
        one_low = elu(one).astype(BF16)
        work[block, net_cols(a_one_at, side)] = one_low
        two = dot(one_low, full[second : second + DET])
        two_low = elu(two).astype(BF16)
        work[block, net_cols(a_two_at, side)] = two_low
        advantage = adv[block][:, 0:1]
        weight = adv[block][:, 1:2]
        if side == 0:
            real = lane_id < ACTIONS
            logits = jnp.where(real, dot_nt(two_low, r.head_pad[...]), -1e30)
            shifted = logits - jnp.max(logits, axis=-1, keepdims=True)
            powers = jnp.where(real, jnp.exp(shifted), 0.0)
            norm = jnp.sum(powers, axis=-1, keepdims=True)
            log_probs = jnp.where(real, shifted - jnp.log(norm), 0.0)
            probs = powers / norm
            taken = act_hot[block].astype(F32)
            chosen = jnp.sum(taken * log_probs, axis=-1, keepdims=True)
            entropy = -jnp.sum(probs * log_probs, axis=-1, keepdims=True)
            r.loss_acc[...] += weight * (-advantage * chosen - entropy_weight * entropy)
            grad_logits = weight * (
                -advantage * (taken - probs) + entropy_weight * probs * (log_probs + entropy)
            )
            both = grad_logits.astype(BF16)
            out_grads[block] = both
            back = dot(both, r.head_pad[...])
        else:
            value = jnp.sum(two_low.astype(F32) * critic_row, axis=-1, keepdims=True)
            gap = value - advantage
            r.loss_acc[...] += weight * (0.5 * gap * gap)
            value_low = (weight * gap).astype(BF16).astype(F32)
            out_grads[block] = jnp.where(lane_id == ACTIONS, value_low, out_grads[block].astype(F32)).astype(BF16)
            back = value_low * critic_row
        back_low = (back * elu_grad(two)).astype(BF16)
        work[block, net_cols(g_two, side)] = back_low
        low_one = (dot_nt(back_low, full[second : second + DET]) * elu_grad(one)).astype(BF16)
        work[block, net_cols(g_one, side)] = low_one
        state_part = dot_nt(low_one, full[first : first + DET])
        if side == 0:
            state_grads[block] = state_part
        else:
            state_grads[block] += state_part

    def net_grads(side):
        base = side * 2048
        for j in range(2):
            part = slice(j * WIDE, (j + 1) * WIDE)
            keep_grads(base + j * WIDE, dot_t(low[:, part], work[:, net_cols(g_one, side)]))
            at = a_one_at + side * DET + j * WIDE
            keep_grads(base + GATES + j * WIDE, dot_t(work[:, at : at + WIDE], work[:, net_cols(g_two, side)]))

        def latent_part(k):
            part = pl.ds(mult(k * WIDE, WIDE), WIDE)
            keep_grads(mult(base + DET + k * WIDE, WIDE), dot(hot_t[part], work[:, net_cols(g_one, side)]))

        each(0, STOCH // WIDE, latent_part)

    blocks = total // BLOCK
    each(0, blocks, lambda k: net_step(k, 0))
    net_grads(0)
    each(0, net_items, heads_rs.to_pair)
    net_step(0, 1)
    each(0, net_items, heads_rs.to_b)
    each(1, blocks, lambda k: net_step(k, 1))
    net_grads(1)
    each(net_items, items, heads_rs.to_pair)

    small = r.small
    head_grad = dot_t(out_grads[...], work[:, a_two_at : a_two_at + 2 * DET])
    small[SM_ACTOR : SM_ACTOR + 24] = head_grad[0:24, 0:WIDE]
    small[SM_ACTOR + 24 : SM_ACTOR + 48] = head_grad[0:24, WIDE:DET]
    small[SM_CRITIC : SM_CRITIC + 1] = head_grad[ACTIONS : ACTIONS + 1, DET : DET + WIDE]
    small[SM_CRITIC + 1 : SM_CRITIC + 2] = head_grad[ACTIONS : ACTIONS + 1, DET + WIDE :]
    small[SM_LOSS : SM_LOSS + 1, 0:128] = jnp.sum(r.loss_acc[...], axis=0, keepdims=True)

    scan_b = 2

    def heads_b(index):
        share = -(-net_items // scan_b)
        low_item = net_items + index * share
        each(low_item, jnp.minimum(low_item + share, items), heads_rs.to_b)

    gain_acc, bias_acc = r.gain_acc, r.bias_acc
    gain_acc[...] = jnp.zeros((8, GATES), F32)
    bias_acc[...] = jnp.zeros((8, GATES), F32)
    carry_ref = r.carry
    carry_ref[...] = state_grads[steps_rows:total]
    work[steps_rows:total, 0 : 4 * DET] = jnp.zeros((total - steps_rows, 4 * DET), BF16)
    gain_mid, bias_mid = gain[:, DET : 2 * DET], bias[:, DET : 2 * DET]

    def fold(value):
        out = value[0:8]
        for k in range(1, cap // 8):
            out = out + value[8 * k : 8 * (k + 1)]
        return out

    def backward_step(index):
        t = horizon - 2 - index
        block = pl.ds(mult(t * cap, 16), cap)
        carry = carry_ref[...]
        normed = raw[block]
        inv_std = inv_ref[block][:, 0:1]
        reset = jax.nn.sigmoid(normed[:, :DET] * gain[:, :DET] + bias[:, :DET])
        update = update_ref[block]
        state = states_ref[block]
        middle = normed[:, DET : 2 * DET] * gain_mid + bias_mid
        candidate = jnp.tanh(reset * middle)
        inner = carry * update * (1.0 - candidate * candidate)
        part = jnp.concatenate(
            [
                inner * middle * reset * (1.0 - reset),
                inner * reset,
                carry * (candidate - state) * update * (1.0 - update),
            ],
            axis=-1,
        )
        gain_acc[...] += fold(part * normed)
        bias_acc[...] += fold(part)
        normed_grad = part * gain
        raw_grad = inv_std * (
            normed_grad
            - jnp.mean(normed_grad, axis=-1, keepdims=True)
            - normed * jnp.mean(normed_grad * normed, axis=-1, keepdims=True)
        )
        grad_low = raw_grad.astype(BF16)
        work[block, 0:GATES] = grad_low
        carry_ref[...] = carry * (1.0 - update) + dot(grad_low, w_back[...]) + state_grads[block]
        pl.when(index < scan_b)(lambda: heads_b(index))
        pl.when((index >= scan_b) & (index % 2 == 0))(lambda: heads_rs.tick((index - scan_b) // 2))

    each(0, horizon - 1, backward_step)

    back_begin, back_finish, back_drain = exchange(DET, r.bk_send, r.bk_recv)
    out_drain()
    start_grads = carry_ref[...].astype(BF16)

    def back_lanes(k):
        block = pl.ds(mult(k * tall, 16), tall)
        r.sent[block, :DET] = dot(r.placing[block][:, 0:cap], start_grads).astype(BF16)

    each(0, lanes // tall, back_lanes)
    back_begin()

    each(0, items, heads_rs.drain_early)
    pl.semaphore_signal(r.credit, inc=1, device_id=(me, sibling), device_id_type=MESH)
    scan_ticks = (horizon - 1 - scan_b + 1) // 2
    tail_ticks = max(rs_ticks - scan_ticks, 0)

    def gru_part(j):
        source = inputs if j < 2 else low
        part = slice((j % 2) * WIDE, (j % 2 + 1) * WIDE)
        for k in range(3):
            value = dot_t(source[:, part], work[:, DET * k : DET * (k + 1)])
            for c in range(4):
                grads[c, pl.ds(ROW_GRU + k + 768 * j, WIDE, stride=3), :] = value[:, 128 * c : 128 * (c + 1)]

    def heads_ticks(low_share, high_share):
        each(
            scan_ticks + tail_ticks * low_share // 4,
            scan_ticks + tail_ticks * high_share // 4,
            heads_rs.tick,
        )

    for j in (3, 2, 1):
        gru_part(j)
    pl.semaphore_wait(r.credit, 1)
    each(0, net_items, gru_rs.to_pair)

    def pre_back(k):
        block = pl.ds(mult(k * pre_block, 16), pre_block)
        value = dot_nt(work[block, 0:GATES], w_gru[0:DET])
        work[block, p_low : p_low + DET] = (value * elu_grad(pre[block])).astype(BF16)

    each(0, pre_blocks, pre_back)
    each(0, net_items, gru_rs.to_b)
    heads_ticks(0, 1)
    gru_part(0)

    def win_part(k):
        part = pl.ds(mult(k * WIDE, WIDE), WIDE)
        keep_grads(mult(k * WIDE, WIDE), dot(hot_t[part], work[:, p_low : p_low + DET]))

    each(0, STOCH // WIDE, win_part)
    each(net_items, items, gru_rs.to_pair)
    heads_ticks(1, 2)
    each(net_items, items, gru_rs.to_b)
    embed_grad = dot_t(act_hot[...], work[:, p_low : p_low + DET])
    small[SM_EMBED : SM_EMBED + 24] = embed_grad[0:24, 0:WIDE]
    small[SM_EMBED + 24 : SM_EMBED + 48] = embed_grad[0:24, WIDE:DET]
    gain_sum = jnp.sum(gain_acc[...], axis=0, keepdims=True)
    bias_sum = jnp.sum(bias_acc[...], axis=0, keepdims=True)
    for k in range(GATES // WIDE):
        small[SM_GAIN + k : SM_GAIN + k + 1] = gain_sum[:, k * WIDE : (k + 1) * WIDE]
        small[SM_BIAS + k : SM_BIAS + k + 1] = bias_sum[:, k * WIDE : (k + 1) * WIDE]

    small_in, scattered = r.small_in, r.scattered
    summed = small_in
    swap_small = remote(small, small_in, r.pair_sem.at[2], r.pair_sem.at[3], me, sibling)
    swap_small.start()
    heads_ticks(2, 4)
    each(0, items, heads_rs.drain)
    each(0, 2, gru_rs.tick)
    swap_small.wait()
    small_sum = small
    small_sum[...] = small[...] + small_in[...]

    def eight(k):
        return pl.ds(mult(k * 8, 8), 8)

    def scatter_copy(k):
        peer = (me + k) % n
        return remote(small_sum.at[eight(peer)], scattered.at[me], r.sc_send.at[k], r.sc_recv.at[k], peer)

    def scatter_landing(k):
        peer = (me + n - k) % n
        return remote(small_sum.at[eight(me)], scattered.at[peer], r.sc_send.at[k], r.sc_recv.at[k], peer)

    def summed_copy(k):
        peer = (me + k) % n
        return remote(summed.at[eight(me)], summed.at[eight(me)], r.sm_send.at[k], r.sm_recv.at[k], peer)

    def summed_landing(k):
        peer = (me + n - k) % n
        return remote(summed.at[eight(peer)], summed.at[eight(peer)], r.sm_send.at[k], r.sm_recv.at[k], peer)

    scattered[me] = small_sum[eight(me)]
    each(1, n, lambda k: scatter_copy(k).start())
    each(2, 4, gru_rs.tick)
    each(1, n, lambda k: scatter_landing(k).wait_recv())
    block_sum = scattered[0]
    for k in range(1, n):
        block_sum = block_sum + scattered[k]
    summed[eight(me)] = block_sum
    each(1, n, lambda k: summed_copy(k).start())
    each(4, rs_ticks, gru_rs.tick)

    back_finish()
    r.start_grad[...] = jnp.zeros((slots, DET), F32)

    def frames(k):
        block = pl.ds(mult(k * tall, 16), tall)
        r.start_grad[...] += dot_t(r.to_lane[block], r.got[block][:, 0:DET])

    each(0, lanes // tall, frames)
    each(1, n, lambda k: summed_landing(k).wait_recv())
    r.loss[...] = summed[SM_LOSS : SM_LOSS + 1, 0:1]
    r.embed_grad[:, 0:WIDE] = summed[SM_EMBED : SM_EMBED + ACTIONS]
    r.embed_grad[:, WIDE:DET] = summed[SM_EMBED + 24 : SM_EMBED + 24 + ACTIONS]
    for k in range(GATES // WIDE):
        for h in range(2):
            lanes_of = slice(h * 128, (h + 1) * 128)
            r.gain_grad[2 * k + h : 2 * k + h + 1] = summed[SM_GAIN + k : SM_GAIN + k + 1, lanes_of]
            r.bias_grad[2 * k + h : 2 * k + h + 1] = summed[SM_BIAS + k : SM_BIAS + k + 1, lanes_of]
    for k in range(2):
        for h in range(2):
            lanes_of = slice(h * 128, (h + 1) * 128)
            r.critic_grad[2 * k + h : 2 * k + h + 1] = summed[SM_CRITIC + k : SM_CRITIC + k + 1, lanes_of]
    r.actor_grad[:, 0:WIDE] = summed[SM_ACTOR : SM_ACTOR + ACTIONS]
    r.actor_grad[:, WIDE:DET] = summed[SM_ACTOR + 24 : SM_ACTOR + 24 + ACTIONS]
    each(0, items, gru_rs.drain_early)
    each(0, items, gru_rs.drain)

    back_drain()
    each(1, n, lambda k: moments_copy(k).wait_send())
    each(1, n, lambda k: scatter_copy(k).wait_send())
    each(1, n, lambda k: summed_copy(k).wait_send())


def on_device(
    start_deter,
    frame_mask,
    counts,
    route,
    weights_flat,
    act_embed,
    gru_gain,
    gru_bias,
    actor_head,
    critic_head,
    latent_idx,
    action_idx,
    rewards,
):
    n = lax.axis_size("dp")
    slots = start_deter.shape[0]
    cap, horizon = action_idx.shape
    shard = weights_flat.shape[0]
    plan = Plan(n, slots, cap, horizon, shard * n // DET)
    total, steps_rows, lanes = plan.all_rows, plan.step_rows, n * plan.lane
    line, half, parts, prow, items = plan.line, plan.half, plan.parts, plan.part_rows, plan.items
    inputs = dict(
        start_deter=start_deter,
        frame_mask=frame_mask.reshape(1, slots),
        counts=counts.reshape(1, 1),
        route=route.reshape(1, slots),
        weights=weights_flat.reshape(plan.rows * 4, 128),
        act_embed=act_embed,
        gain=gru_gain.reshape(GATES // 128, 128),
        bias=gru_bias.reshape(GATES // 128, 128),
        actor_head=actor_head.T,
        critic_head=critic_head.reshape(DET // 128, 128),
        latent=jnp.transpose(latent_idx, (1, 2, 0)),
        action=action_idx.T,
        rewards=rewards.T,
    )
    outputs = dict(
        loss=(1, 1),
        start_grad=(slots, DET),
        weights_grad=(plan.rows * 4, 128),
        embed_grad=(ACTIONS, DET),
        gain_grad=(GATES // 128, 128),
        bias_grad=(GATES // 128, 128),
        actor_grad=(ACTIONS, DET),
        critic_grad=(DET // 128, 128),
    )
    group_rows = half * 4 * plan.rows
    half_rows = group_rows // 2
    scratch = dict(
        narrow=((plan.rows * 2, 128), F32),
        latent_row=((LATENTS, total), F32),
        action_row=((1, total), F32),
        returns=((1, total), F32),
        weight_row=((1, total), F32),
        kept=((2 * items, prow, DET), F32),
        full=((n * plan.rows, DET), BF16),
        start=((128, DET + META), F32),
        to_lane=((lanes, slots), BF16),
        sent=((lanes, DET + META), BF16),
        got=((lanes, DET + META), BF16),
        placing=((lanes, 128), BF16),
        hot=((total, STOCH), BF16),
        hot_t=((STOCH, total), BF16),
        act_hot=((total, 128), BF16),
        embed_pad=((32, DET), BF16),
        head_pad=((128, DET), BF16),
        small=((plan.small, WIDE), F32),
        small_in=((plan.small, WIDE), F32),
        scattered=((n, 8, WIDE), F32),
        states=((total, DET), F32),
        adv=((total, 128), F32),
        pair=((2, 8, 128), F32),
        moments=((n, 8, 128), F32),
        shuffle=((TALL, TALL), BF16),
        w_gru=((STOCH, GATES), BF16),
        pre=((steps_rows, DET), F32),
        inputs=((total, DET), BF16),
        work=((total, 8 * DET), BF16),
        raw=((steps_rows, GATES), F32),
        low=((total, DET), BF16),
        update=((steps_rows, DET), F32),
        inv=((steps_rows, 128), F32),
        out_grads=((total, 128), BF16),
        state_grads=((total, DET), F32),
        loss_acc=((BLOCK, 128), F32),
        grads=((4, group_rows, 128), F32),
        pair_in=((half_rows, DET), BF16),
        b_in=((2, half_rows // 2, DET), BF16),
        a_in=((2, half_rows // 4, DET), BF16),
        z_in=((2, half_rows // 4, DET), BF16),
        gain_acc=((8, GATES), F32),
        bias_acc=((8, GATES), F32),
        carry=((cap, DET), F32),
    )
    semaphores = dict(
        ex_send=(n,),
        ex_recv=(n,),
        bk_send=(n,),
        bk_recv=(n,),
        mo_send=(n,),
        mo_recv=(n,),
        sc_send=(n,),
        sc_recv=(n,),
        sm_send=(n,),
        sm_recv=(n,),
        pair_sem=(4,),
        ag_recv=(n, parts),
        sh_recv=(n, parts),
        far_send=(parts,),
        line_send=(line, parts, max(plan.bits - 1, 1)),
        a_send=(line, parts),
        b_send=(line, parts, 2),
        sh_send=(line, parts, 4),
        pair_s=(2, half, parts),
        pair_r=(2, half, parts),
        b_s=(2, half, parts),
        b_r=(2, half, parts),
        a_s=(2, half, parts),
        a_r=(2, half, parts),
        z_s=(2, half, parts),
        z_r=(2, half, parts),
        fin_s=(parts,),
        fin_r=(parts,),
    )
    names = list(inputs) + list(outputs) + list(scratch) + list(semaphores) + list(dict(credit=0))
    vmem = pl.BlockSpec(memory_space=pltpu.VMEM)
    found = pl.pallas_call(
        functools.partial(kernel_body, plan, names),
        out_shape=[jax.ShapeDtypeStruct(shape, F32) for shape in outputs.values()],
        in_specs=[vmem] * len(inputs),
        out_specs=[vmem] * len(outputs),
        scratch_shapes=[pltpu.VMEM(shape, dtype) for shape, dtype in scratch.values()]
        + [pltpu.SemaphoreType.DMA(shape) for shape in semaphores.values()]
        + [pltpu.SemaphoreType.REGULAR],
        compiler_params=pltpu.CompilerParams(
            collective_id=0, has_side_effects=True, vmem_limit_bytes=127 * 2**19
        ),
    )(*inputs.values())
    loss, start_grad, weights_grad, embed_grad, gain_grad, bias_grad, actor_grad, critic_grad = found
    return (
        loss.reshape(()),
        start_grad,
        weights_grad.reshape(shard),
        embed_grad,
        gain_grad.reshape(GATES),
        bias_grad.reshape(GATES),
        actor_grad.T,
        critic_grad.reshape(DET),
    )


def solution(mesh):
    return jax.shard_map(
        on_device,
        mesh=mesh,
        in_specs=(
            P(("dp", "rep"), None),
            P(("dp", "rep")),
            P(("dp", "rep")),
            P(("dp", "rep")),
            P("dp"),
            P(),
            P(),
            P(),
            P(),
            P(),
            P(("dp", "rep"), None, None),
            P(("dp", "rep"), None),
            P(("dp", "rep"), None),
        ),
        out_specs=(P(), P(("dp", "rep"), None), P("dp"), P(), P(), P(), P(), P()),
        check_vma=False,
    )
```

time: 1610 us -> 168 us (0.10)
  blocking collectives: 805 us -> 0 us
  matrix products: 280 us -> 0 us
  other arithmetic: 255 us -> 0 us
  local copies, waits for them, and re-layouts: 207 us -> 7.13 us
  Pallas kernels: 0 us -> 157 us
  starting transfers between devices: 19.9 us -> 0 us
  between operations: 21.9 us -> 3.05 us
    unnamed x1 -> x0, blocking collectives: 721 us -> none
    dot_general x236 -> x0, matrix products: 280 us -> none  [the longest x138 128 us: product(): return jnp.dot(left, right, preferred_element_type=jnp.float32)]
    pallas_call x0 -> x1, Pallas kernels: none -> 157 us  [on_device(): pl.pallas_call(functools.partial(kernel_body, plan, names), out_shape=[ja...]
    reduce_sum x130 -> x0, other arithmetic: 105 us -> none  [the longest x60 39.3 us: gru_update(): jnp.mean(centred * centred, axis=-1, keepdims=True) + norm_eps]
    psum x2 -> x0, blocking collectives: 84.2 us -> none  [the longest x1 45.3 us: on_device(): lax.psum((jnp.sum(weight_mask * returns), jnp.sum(weight_mask * returns *...]
    dynamic_update_slice x120 -> x0, local copies, waits for them, and re-layouts: 67.1 us -> none  [the longest x60 38.7 us: forward_micro(): lax.scan(dyn_step, start_h, (latent_block[:-1], action_block[:-1]))]
    slice x24 -> x0, local copies, waits for them, and re-layouts: 53.4 us -> none  [the longest x6 27.6 us: on_device(): latent_block = jnp.swapaxes(latent_hot[span_lo:span_hi], 0, 1)]
    dynamic_update_slice x30 -> x0, other arithmetic: 49.5 us -> none  [backward_micro(): lax.scan(back_step, state_grad[-1], (states, pre_acts, gru_raws, state_gr...]
  transfers between devices with their start and end apart: 5 -> 0, of which waited for: 1 -> 0; matrix products, arithmetic and copies ran while one was open for 8% -> 0% of each run, Pallas kernels for 0% -> 0%
where the time goes in v1:
time: 168 us
  Pallas kernels  157 us (93%)
  local copies, waits for them, and re-layouts  7.13 us (4%)
  between operations  3.05 us (2%)
    pallas_call x1, Pallas kernels, on_device(): pl.pallas_call(functools.partial(kernel_body, plan, names), out_shape=[ja...  157 us
    unnamed x17, local copies, waits for them, and re-layouts  7.13 us

profile of v1, /device:TPU:0, one launch (start us, length us, event | category | flops | bytes accessed | tf_op | source)
XLA Modules:
  0.0 167.6 jit_solution(8143776343013554159)
XLA Ops:
  1.3 157.4 %shard_map.188 = (f32[1,1]{1,0:T(1,128)}, f32[96,512]{1,0:T(8,128)}, f32[2048,128]{1,0:T(8,128)}, f32[18,512]{1,0:T(8,128)}, f32[12,128]{1,0:T(8,128)}, /*index=...) custom-call(bf16[96,512]{1,0:T(8,128)(2,1)} %refs_0_.1, s32[1,96]{1,0:T(1,128)} %bitcast.31, ...), custom_call_target="tpu_custom_call" | custom-call | tf_op jit(solution)/shard_map/pallas_call | solution.py:1064
  159.3 1.6 copy.31
  161.0 0.0 copy-start.1
  161.0 2.3 %copy.32 = f32[262144]{0:T(1024)} copy(f32[262144]{0:T(1024)} %bitcast.18) | data formatting | bytes 2097152
  163.2 0.0 copy-done.1
  163.2 0.0 copy-start.3
  163.2 0.0 copy-start
  163.2 0.6 copy.33
  163.9 0.1 copy-done.3
  163.9 0.0 copy-start.2
  163.9 0.6 copy.34
  164.5 0.1 copy-done.2
  164.6 0.6 copy.35
  165.2 0.0 copy-done
  165.2 0.0 copy-start.4
  165.2 0.6 copy.36
  165.9 0.0 copy-done.4
  165.9 0.6 copy.37
Async XLA Ops:
  161.0 2.3 %copy-start.1 = (f32[18,512]{1,0:T(8,128)S(1)}, f32[18,512]{1,0:T(8,128)}, u32[]{:S(2)}) copy-start(f32[18,512]{1,0:T(8,128)} %get-tuple-element.35) | copy-start | bytes 110596
  163.2 0.7 copy-start.3
  163.2 2.0 %copy-start = (f32[18,512]{1,0:T(8,128)S(1)}, f32[18,512]{1,0:T(8,128)}, u32[]{:S(2)}) copy-start(f32[18,512]{1,0:T(8,128)} %get-tuple-element.22) | copy-start | bytes 110596
  163.9 0.7 copy-start.2
  165.2 0.7 copy-start.4

commit v2 on v1

--- a/solution.py
+++ b/solution.py
@@ -18,7 +18,9 @@
 META = 128
 BLOCK = 192
 TALL = 384
-LAG_A, LAG_B, LAG_Z = 2, 4, 1
+LAG_A, LAG_B, LAG_Z = 2, 4, 2
+SMALL_TICKS = 4
+START_TICKS = 3
 
 discount = 0.99
 entropy_weight = 0.1
@@ -198,13 +200,14 @@
         return me + 4 * 2**b * (1 - 2 * bit_of(z, b))
 
     def item_at(i):
-        group = i // items
-        inner = i % items
-        order = inner // parts
+        spot = i // parts
+        late = jnp.where(z < half, spot, jnp.where(spot == 0, half, spot - 1 + spot // (half + 1)))
+        group = late // half
+        order = late % half
         place = z % half
         for b in range(bits - 1):
             place = place + bit_of(order, b) * 2**b * (1 - 2 * bit_of(z, b))
-        return group, order, group * half + place, inner % parts
+        return order, group * half + place, i % parts
 
     def full_at(shard, piece, part):
         return full.at[pl.ds(mult(shard * rows + part * (rows // 2) + piece * prow, 16), prow)]
@@ -236,7 +239,7 @@
         ]
 
     def gather_line(i):
-        _, order, zi, piece = item_at(i)
+        order, zi, piece = item_at(i)
 
         @pl.when(zi != z)
         def _():
@@ -250,24 +253,27 @@
         share_copy(zi * 4 + q, piece, r.sh_send.at[zi, piece, 0]).start()
 
     def gather_a(i):
-        _, _, zi, piece = item_at(i)
+        _, zi, piece = item_at(i)
         gather_copy(zi * 4 + q_a, piece, r.a_send.at[zi, piece], me).wait_recv()
         plane_sends(zi, piece)[2].start()
         share_copy(zi * 4 + q_a, piece, r.sh_send.at[zi, piece, 1]).start()
 
     def gather_b(i):
-        _, _, zi, piece = item_at(i)
+        _, zi, piece = item_at(i)
         for k, where in ((2, q_b), (3, q_ab)):
             gather_copy(zi * 4 + where, piece, r.a_send.at[zi, piece], me).wait_recv()
             share_copy(zi * 4 + where, piece, r.sh_send.at[zi, piece, k]).start()
 
     def gather_shared(i):
-        _, _, zi, piece = item_at(i)
+        zi, piece = i // parts, i % parts
         for k, where in ((0, q), (1, q_a), (2, q_b), (3, q_ab)):
             share_copy(zi * 4 + where, piece, r.sh_send.at[zi, piece, k], sibling).wait_recv()
 
     def gather_drain(i):
-        _, order, zi, piece = item_at(i)
+        zi, piece = i // parts, i % parts
+        place, order = zi % half, 0
+        for b in range(bits - 1):
+            order = order + 2**b * ((bit_of(place, b) + bit_of(z, b)) % 2)
         for need, copy in line_sends(order, zi, piece):
             pl.when(need)(copy.wait_send)
         for copy in plane_sends(zi, piece):
@@ -278,7 +284,7 @@
     lag_a, lag_b = LAG_A, LAG_B
     all_items = 2 * items
     ticks = all_items + lag_b
-    first_ticks = items + lag_b
+    first_ticks = items + lag_b + jnp.where(z < half, 0, parts)
 
     def gather_tick(k):
         pl.when(k < all_items)(lambda: gather_line(k))
@@ -286,9 +292,8 @@
         pl.when((k >= lag_b) & (k < all_items + lag_b))(lambda: gather_b(k - lag_b))
 
     each(0, parts, lambda piece: far_copy(piece).start())
-    early = min(2, first_ticks)
+    early = min(2, START_TICKS, items)
     each(0, early, gather_tick)
-    out_begin()
 
     hot, hot_t, act_hot = r.hot, r.hot_t, r.act_hot
     for t in range(horizon):
@@ -319,7 +324,46 @@
     r.head_pad[0:ACTIONS] = r.actor_head[...]
     r.small[...] = jnp.zeros(r.small.shape, F32)
 
-    each(early, first_ticks, gather_tick)
+    middle_ticks = min(START_TICKS, items + lag_b)
+    each(early, middle_ticks, gather_tick)
+    out_begin()
+    each(middle_ticks, first_ticks, gather_tick)
+
+    each(0, items, gather_shared)
+
+    shuffle = r.shuffle
+    row_i = iota((TALL, TALL), 0)
+    shuffle[...] = jnp.where(
+        iota((TALL, TALL), 1) == 3 * (row_i % 128) + row_i // 128, 1.0, 0.0
+    ).astype(BF16)
+    w_gru = r.w_gru
+    for j in range(8):
+        block = full[ROW_GRU + TALL * j : ROW_GRU + TALL * (j + 1)]
+        sorted_rows = dot(shuffle[...], block).astype(BF16)
+        for k in range(3):
+            w_gru[128 * j : 128 * (j + 1), DET * k : DET * (k + 1)] = sorted_rows[128 * k : 128 * (k + 1)]
+    each(0, items, gather_drain)
+    each(0, parts, lambda piece: pl.when(z < half)(far_copy(piece).wait_send))
+    w_back = full.at[ROW_GRU : ROW_GRU + GATES]
+    pre, inputs, raw = r.pre, r.inputs, r.raw
+    low, work = r.low, r.work
+    a_one_at, a_two_at, g_one, g_two = 0, 2 * DET, 4 * DET, 6 * DET
+    p_low = GATES
+    inputs[steps_rows:total] = jnp.zeros((total - steps_rows, DET), BF16)
+    pre_block = 5 * cap
+
+    def pre_step(k):
+        block = pl.ds(mult(k * pre_block, 16), pre_block)
+        value = dot(hot[block], full[ROW_WIN : ROW_WIN + STOCH])
+        value = value + dot(act_hot[block][:, 0:32], r.embed_pad[...])
+        pre[block] = value
+        active = elu(value).astype(BF16)
+        inputs[block] = active
+        raw[block] = dot(active, w_gru[0:DET])
+        gather_tick(first_ticks + k)
+
+    pre_blocks = (horizon - 1) // 5
+    each(0, pre_blocks, pre_step)
 
     out_finish()
     r.start[...] = jnp.zeros((128, DET + META), F32)
@@ -362,7 +406,6 @@
     pair[0] = sums
     swap = remote(pair.at[0], pair.at[1], r.pair_sem.at[0], r.pair_sem.at[1], me, sibling)
     swap.start()
-    each(0, items, gather_shared)
     swap.wait()
     moments[me] = pair[0] + pair[1]
 
@@ -375,46 +418,6 @@
         return remote(moments.at[peer], moments.at[peer], r.mo_send.at[k], r.mo_recv.at[k], peer)
 
     each(1, n, lambda k: moments_copy(k).start())
-
-    shuffle = r.shuffle
-    row_i = iota((TALL, TALL), 0)
-    shuffle[...] = jnp.where(
-        iota((TALL, TALL), 1) == 3 * (row_i % 128) + row_i // 128, 1.0, 0.0
-    ).astype(BF16)
-    w_gru = r.w_gru
-    for j in range(8):
-        block = full[ROW_GRU + TALL * j : ROW_GRU + TALL * (j + 1)]
-        sorted_rows = dot(shuffle[...], block).astype(BF16)
-        for k in range(3):
-            w_gru[128 * j : 128 * (j + 1), DET * k : DET * (k + 1)] = sorted_rows[128 * k : 128 * (k + 1)]
-    each(0, items, gather_drain)
-    each(0, parts, lambda piece: pl.when(z < half)(far_copy(piece).wait_send))
-    w_back = full.at[ROW_GRU : ROW_GRU + GATES]
-    for j in range(4):
-        for k in range(3):
-            w_back[DET * k : DET * (k + 1), 128 * j : 128 * (j + 1)] = w_gru[
-                DET + 128 * j : DET + 128 * (j + 1), DET * k : DET * (k + 1)
-            ].T
-
-    pre, inputs, raw = r.pre, r.inputs, r.raw
-    low, work = r.low, r.work
-    a_one_at, a_two_at, g_one, g_two = 0, 2 * DET, 4 * DET, 6 * DET
-    p_low = GATES
-    inputs[steps_rows:total] = jnp.zeros((total - steps_rows, DET), BF16)
-    pre_block = 5 * cap
-
-    def pre_step(k):
-        block = pl.ds(mult(k * pre_block, 16), pre_block)
-        value = dot(hot[block], full[ROW_WIN : ROW_WIN + STOCH])
-        value = value + dot(act_hot[block][:, 0:32], r.embed_pad[...])
-        pre[block] = value
-        active = elu(value).astype(BF16)
-        inputs[block] = active
-        raw[block] = dot(active, w_gru[0:DET])
-        gather_tick(first_ticks + k)
-
-    pre_blocks = (horizon - 1) // 5
-    each(0, pre_blocks, pre_step)
 
     def as_row(ref):
         value = ref[...].astype(F32)
@@ -441,11 +444,15 @@
         update = jax.nn.sigmoid(mixed[:, 2 * DET :] - 1.0)
         update_ref[block] = update
         states_ref[pl.ds(mult(t * cap + cap, 16), cap)] = update * candidate + (1.0 - update) * state
+        j, k = t % 12 // 3, t % 3
+        w_back[pl.ds(mult(DET * k, DET), DET), pl.ds(mult(128 * j, 128), 128)] = w_gru[
+            pl.ds(mult(DET + 128 * j, 128), 128), pl.ds(mult(DET * k, DET), DET)
+        ].T
         pl.when(t % 3 == 2)(lambda: gather_tick(first_ticks + pre_blocks + t // 3))
 
     each(0, horizon - 1, forward_step)
     done_ticks = first_ticks + pre_blocks + (horizon - 1) // 3
-    each(done_ticks, max(ticks, done_ticks), gather_tick)
+    each(done_ticks, jnp.maximum(ticks, done_ticks), gather_tick)
     low[steps_rows:total] = states_ref[steps_rows:total].astype(BF16)
     each(items, 2 * items, gather_shared)
     each(items, 2 * items, gather_drain)
@@ -594,6 +601,8 @@
             t, piece = self.target(i)
             self.b_copy(t, piece).wait_recv()
             other = 1 - a_bit
+            if self.group == 0:
+                heads_rs.a_copy(t, piece).wait_send()
             full[self.out_rows(t, 3 * rows, piece, 1)] = (
                 self.load(t, piece, other) + self.b_part(t, piece, other)
             ).astype(BF16)
@@ -621,6 +630,8 @@
 
                     @pl.when(self.differs(b, t))
                     def _():
+                        if self.group == 0:
+                            heads_rs.plane_gone(t, piece)
                         full[self.out_rows(t, 3 * rows + rows // 2, piece, 1)] = value.astype(BF16)
                         self.z_copy(b, t, piece).start()
 
@@ -631,26 +642,40 @@
             self.pair_copy(t, piece).wait_send()
             self.b_copy(t, piece).wait_send()
 
+        def plane_gone(self, t, piece):
+            for b in range(bits):
+                pl.when(self.holds(b, t) & self.differs(b, t))(self.z_copy(b, t, piece).wait_send)
+
         def drain(self, i):
             t, piece = self.target(i)
-            self.a_copy(t, piece).wait_send()
-            for b in range(bits):
-                pl.when(self.holds(b, t) & self.differs(b, t))(self.z_copy(b, t, piece).wait_send)
+            if self.group == 0:
+                self.a_copy(t, piece).wait_send()
+                self.plane_gone(t, piece)
+            else:
+                for b in range(bits):
+                    waited = False
+                    for c in range(bits):
+                        waited = waited | (gru_rs.holds(c, t) & gru_rs.differs(c, t))
+                    pl.when(self.holds(b, t) & self.differs(b, t) & ~waited)(self.z_copy(b, t, piece).wait_send)
 
             @pl.when(self.holds(bits, t))
             def _():
                 self.fin_copy(piece).wait_send()
                 self.fin_copy(piece, sibling).wait_recv()
 
-        def tick(self, k):
-            pl.when((k >= 0) & (k < items))(lambda: self.to_a(k))
-            for b in range(bits + 1):
-                j = k - LAG_Z * (b + 1)
-                pl.when((j >= 0) & (j < items))(lambda b=b, j=j: self.to_plane(b, j))
-
-    rs_ticks = items + LAG_Z * (bits + 1)
     heads_rs, gru_rs = Reducer(1), Reducer(0)
     net_items = items // 2
+
+    def of_item(k, stage):
+        pl.when((k >= 0) & (k < items))(lambda: stage(heads_rs, k))
+        pl.when((k >= items) & (k < 2 * items))(lambda: stage(gru_rs, k - items))
+
+    def rs_tick(k):
+        of_item(k, lambda rs, i: rs.to_a(i))
+        for b in range(bits + 1):
+            of_item(k - LAG_Z * (b + 1), lambda rs, i, b=b: rs.to_plane(b, i))
+
+    rs_ticks = 2 * items + LAG_Z * (bits + 1)
 
     out_grads, state_grads = r.out_grads, r.state_grads
     r.loss_acc[...] = jnp.zeros((BLOCK, 128), F32)
@@ -730,8 +755,10 @@
     net_step(0, 1)
     each(0, net_items, heads_rs.to_b)
     each(1, blocks, lambda k: net_step(k, 1))
+    each(0, net_items // 2, rs_tick)
     net_grads(1)
     each(net_items, items, heads_rs.to_pair)
+    each(net_items // 2, net_items, rs_tick)
 
     small = r.small
     head_grad = dot_t(out_grads[...], work[:, a_two_at : a_two_at + 2 * DET])
@@ -747,6 +774,8 @@
         share = -(-net_items // scan_b)
         low_item = net_items + index * share
         each(low_item, jnp.minimum(low_item + share, items), heads_rs.to_b)
+
+    scan_ticks = net_items + (horizon - 1) // 3 - 1
 
     gain_acc, bias_acc = r.gain_acc, r.bias_acc
     gain_acc[...] = jnp.zeros((8, GATES), F32)
@@ -794,7 +823,7 @@
         work[block, 0:GATES] = grad_low
         carry_ref[...] = carry * (1.0 - update) + dot(grad_low, w_back[...]) + state_grads[block]
         pl.when(index < scan_b)(lambda: heads_b(index))
-        pl.when((index >= scan_b) & (index % 2 == 0))(lambda: heads_rs.tick((index - scan_b) // 2))
+        pl.when((index >= scan_b) & (index % 3 == 1))(lambda: rs_tick(net_items + index // 3 - 1))
 
     each(0, horizon - 1, backward_step)
 
@@ -811,9 +840,6 @@
 
     each(0, items, heads_rs.drain_early)
     pl.semaphore_signal(r.credit, inc=1, device_id=(me, sibling), device_id_type=MESH)
-    scan_ticks = (horizon - 1 - scan_b + 1) // 2
-    tail_ticks = max(rs_ticks - scan_ticks, 0)
-
     def gru_part(j):
         source = inputs if j < 2 else low
         part = slice((j % 2) * WIDE, (j % 2 + 1) * WIDE)
@@ -822,13 +848,6 @@
             for c in range(4):
                 grads[c, pl.ds(ROW_GRU + k + 768 * j, WIDE, stride=3), :] = value[:, 128 * c : 128 * (c + 1)]
 
-    def heads_ticks(low_share, high_share):
-        each(
-            scan_ticks + tail_ticks * low_share // 4,
-            scan_ticks + tail_ticks * high_share // 4,
-            heads_rs.tick,
-        )
-
     for j in (3, 2, 1):
         gru_part(j)
     pl.semaphore_wait(r.credit, 1)
@@ -840,8 +859,10 @@
         work[block, p_low : p_low + DET] = (value * elu_grad(pre[block])).astype(BF16)
 
     each(0, pre_blocks, pre_back)
+    ready = min(scan_ticks, items)
+    each(ready, items, rs_tick)
+    ready = max(ready, items)
     each(0, net_items, gru_rs.to_b)
-    heads_ticks(0, 1)
     gru_part(0)
 
     def win_part(k):
@@ -850,8 +871,11 @@
 
     each(0, STOCH // WIDE, win_part)
     each(net_items, items, gru_rs.to_pair)
-    heads_ticks(1, 2)
+    step_ticks = max(net_items // 4, 1)
+    each(ready, ready + step_ticks, rs_tick)
     each(net_items, items, gru_rs.to_b)
+    each(ready + step_ticks, ready + 2 * step_ticks, rs_tick)
+    ready += 2 * step_ticks
     embed_grad = dot_t(act_hot[...], work[:, p_low : p_low + DET])
     small[SM_EMBED : SM_EMBED + 24] = embed_grad[0:24, 0:WIDE]
     small[SM_EMBED + 24 : SM_EMBED + 48] = embed_grad[0:24, WIDE:DET]
@@ -865,9 +889,7 @@
     summed = small_in
     swap_small = remote(small, small_in, r.pair_sem.at[2], r.pair_sem.at[3], me, sibling)
     swap_small.start()
-    heads_ticks(2, 4)
-    each(0, items, heads_rs.drain)
-    each(0, 2, gru_rs.tick)
+    each(ready, ready + step_ticks, rs_tick)
     swap_small.wait()
     small_sum = small
     small_sum[...] = small[...] + small_in[...]
@@ -893,14 +915,16 @@
 
     scattered[me] = small_sum[eight(me)]
     each(1, n, lambda k: scatter_copy(k).start())
-    each(2, 4, gru_rs.tick)
+    landing = max(ready + step_ticks, rs_ticks - SMALL_TICKS)
+    each(ready + step_ticks, landing, rs_tick)
     each(1, n, lambda k: scatter_landing(k).wait_recv())
     block_sum = scattered[0]
     for k in range(1, n):
         block_sum = block_sum + scattered[k]
     summed[eight(me)] = block_sum
     each(1, n, lambda k: summed_copy(k).start())
-    each(4, rs_ticks, gru_rs.tick)
+    each(landing, rs_ticks, rs_tick)
+    each(0, items, heads_rs.drain)
 
     back_finish()
     r.start_grad[...] = jnp.zeros((slots, DET), F32)
@@ -932,6 +956,12 @@
     each(1, n, lambda k: moments_copy(k).wait_send())
     each(1, n, lambda k: scatter_copy(k).wait_send())
     each(1, n, lambda k: summed_copy(k).wait_send())
+
+
+def hand_over(*refs):
+    count = len(refs) // 2
+    for k in range(count):
+        refs[count + k][...] = refs[k][...]
 
 
 def on_device(
@@ -1073,6 +1103,12 @@
             collective_id=0, has_side_effects=True, vmem_limit_bytes=127 * 2**19
         ),
     )(*inputs.values())
+    found = pl.pallas_call(
+        hand_over,
+        out_shape=[jax.ShapeDtypeStruct(shape, F32) for shape in outputs.values()],
+        in_specs=[vmem] * len(outputs),
+        out_specs=[vmem] * len(outputs),
+    )(*found)
     loss, start_grad, weights_grad, embed_grad, gain_grad, bias_grad, actor_grad, critic_grad = found
     return (
         loss.reshape(()),

time: 168 us -> 145 us (0.86)
  Pallas kernels: 157 us -> 144 us
  local copies, waits for them, and re-layouts: 7.13 us -> 0 us
  between operations: 3.05 us -> 1.29 us
    pallas_call x1, Pallas kernels: 157 us -> 141 us  [on_device(): pl.pallas_call(functools.partial(kernel_body, plan, names), out_shape=[ja...]
    unnamed x17 -> x0, local copies, waits for them, and re-layouts: 7.13 us -> none
    pallas_call x0 -> x1, Pallas kernels: none -> 3.03 us  [on_device(): pl.pallas_call(hand_over, out_shape=[jax.ShapeDtypeStruct(shape, F32) for...]
where the time goes in v2:
time: 145 us
  Pallas kernels  144 us (99%)
    pallas_call x1, Pallas kernels, on_device(): pl.pallas_call(functools.partial(kernel_body, plan, names), out_shape=[ja...  141 us
    pallas_call x1, Pallas kernels, on_device(): pl.pallas_call(hand_over, out_shape=[jax.ShapeDtypeStruct(shape, F32) for...  3.03 us

profile of v2, /device:TPU:0, one launch (start us, length us, event | category | flops | bytes accessed | tf_op | source)
XLA Modules:
  0.0 144.9 jit_solution(13734838345405175464)
XLA Ops:
  1.3 140.5 %shard_map.188 = (f32[1,1]{1,0:T(1,128)}, f32[96,512]{1,0:T(8,128)}, f32[2048,128]{1,0:T(8,128)}, f32[18,512]{1,0:T(8,128)}, f32[12,128]{1,0:T(8,128)}, /*index=...) custom-call(bf16[96,512]{1,0:T(8,128)(2,1)} %refs_0_.1, s32[1,96]{1,0:T(1,128)} %bitcast.26, ...), custom_call_target="tpu_custom_call" | custom-call | tf_op jit(solution)/shard_map/pallas_call | solution.py:1094
  141.8 3.0 %shard_map.189 = (f32[1,1]{1,0:T(1,128)}, f32[96,512]{1,0:T(8,128)}, f32[2048,128]{1,0:T(8,128)}, f32[18,512]{1,0:T(8,128)}, f32[12,128]{1,0:T(8,128)}, /*index=...) custom-call(f32[1,1]{1,0:T(1,128)} %get-tuple-element.24.refs_0_, f32[96,512]{1,0:T(8,128)} %get-tuple-element.25.refs_1_, ...), custom_call_target="tpu_custom_call" | custom-call | tf_op jit(solution)/shard_map/pallas_call | solution.py:1106

commit v3 on v2

--- a/solution.py
+++ b/solution.py
@@ -16,10 +16,11 @@
 GATES = 1536
 WIDE = 256
 META = 128
-BLOCK = 192
 TALL = 384
 LAG_A, LAG_B, LAG_Z = 2, 4, 2
-SMALL_TICKS = 4
+GATHER_PARTS = 4
+AHEAD = 4
+SCATTER_TICKS, SPREAD_TICKS = 11, 4
 START_TICKS = 3
 
 discount = 0.99
@@ -79,8 +80,10 @@
         self.parts = max(1, min(4, self.rows // 2 // 32))
         self.part_rows = self.rows // 2 // self.parts
         self.items = self.half * self.parts
+        self.cuts = max(1, min(GATHER_PARTS, self.rows // 2 // 16))
         self.bits = self.line.bit_length() - 1
         self.small = 8 * devices
+        self.block = 256 if self.line <= 4 else 192
 
 
 def kernel_body(plan, names, *refs):
@@ -193,24 +196,29 @@
         return begin, finish, drain
 
     out_begin, out_finish, out_drain = exchange(DET + META, r.ex_send, r.ex_recv)
+    cuts = plan.cuts
+    chunks = half * cuts
+    crow = rows // 2 // cuts
     def bit_of(value, b):
         return (value // 2**b) % 2
 
     def across(b):
         return me + 4 * 2**b * (1 - 2 * bit_of(z, b))
 
+    ahead = min(AHEAD, cuts)
+
     def item_at(i):
-        spot = i // parts
-        late = jnp.where(z < half, spot, jnp.where(spot == 0, half, spot - 1 + spot // (half + 1)))
+        i = jnp.where(z < half, i, jnp.where(i < ahead, chunks + i, jnp.where(i < ahead + chunks, i - ahead, i)))
+        late = i // cuts
         group = late // half
         order = late % half
         place = z % half
         for b in range(bits - 1):
             place = place + bit_of(order, b) * 2**b * (1 - 2 * bit_of(z, b))
-        return order, group * half + place, i % parts
+        return order, group * half + place, i % cuts
 
     def full_at(shard, piece, part):
-        return full.at[pl.ds(mult(shard * rows + part * (rows // 2) + piece * prow, 16), prow)]
+        return full.at[pl.ds(mult(shard * rows + part * (rows // 2) + piece * crow, 16), crow)]
 
     def gather_copy(shard, piece, send, dev):
         view = full_at(shard, piece, core)
@@ -265,12 +273,12 @@
             share_copy(zi * 4 + where, piece, r.sh_send.at[zi, piece, k]).start()
 
     def gather_shared(i):
-        zi, piece = i // parts, i % parts
+        zi, piece = i // cuts, i % cuts
         for k, where in ((0, q), (1, q_a), (2, q_b), (3, q_ab)):
             share_copy(zi * 4 + where, piece, r.sh_send.at[zi, piece, k], sibling).wait_recv()
 
     def gather_drain(i):
-        zi, piece = i // parts, i % parts
+        zi, piece = i // cuts, i % cuts
         place, order = zi % half, 0
         for b in range(bits - 1):
             order = order + 2**b * ((bit_of(place, b) + bit_of(z, b)) % 2)
@@ -282,17 +290,17 @@
             share_copy(zi * 4 + where, piece, r.sh_send.at[zi, piece, k]).wait_send()
 
     lag_a, lag_b = LAG_A, LAG_B
-    all_items = 2 * items
-    ticks = all_items + lag_b
-    first_ticks = items + lag_b + jnp.where(z < half, 0, parts)
+    all_chunks = 2 * chunks
+    ticks = all_chunks + lag_b
+    first_ticks = chunks + lag_b + jnp.where(z < half, 0, ahead)
 
     def gather_tick(k):
-        pl.when(k < all_items)(lambda: gather_line(k))
-        pl.when((k >= lag_a) & (k < all_items + lag_a))(lambda: gather_a(k - lag_a))
-        pl.when((k >= lag_b) & (k < all_items + lag_b))(lambda: gather_b(k - lag_b))
-
-    each(0, parts, lambda piece: far_copy(piece).start())
-    early = min(2, START_TICKS, items)
+        pl.when(k < all_chunks)(lambda: gather_line(k))
+        pl.when((k >= lag_a) & (k < all_chunks + lag_a))(lambda: gather_a(k - lag_a))
+        pl.when((k >= lag_b) & (k < all_chunks + lag_b))(lambda: gather_b(k - lag_b))
+
+    each(0, cuts, lambda piece: far_copy(piece).start())
+    early = min(2, START_TICKS, chunks)
     each(0, early, gather_tick)
 
     hot, hot_t, act_hot = r.hot, r.hot_t, r.act_hot
@@ -324,12 +332,12 @@
     r.head_pad[0:ACTIONS] = r.actor_head[...]
     r.small[...] = jnp.zeros(r.small.shape, F32)
 
-    middle_ticks = min(START_TICKS, items + lag_b)
+    middle_ticks = min(START_TICKS, chunks + lag_b)
     each(early, middle_ticks, gather_tick)
     out_begin()
     each(middle_ticks, first_ticks, gather_tick)
 
-    each(0, items, gather_shared)
+    each(0, chunks, gather_shared)
 
     shuffle = r.shuffle
     row_i = iota((TALL, TALL), 0)
@@ -342,8 +350,6 @@
         sorted_rows = dot(shuffle[...], block).astype(BF16)
         for k in range(3):
             w_gru[128 * j : 128 * (j + 1), DET * k : DET * (k + 1)] = sorted_rows[128 * k : 128 * (k + 1)]
-    each(0, items, gather_drain)
-    each(0, parts, lambda piece: pl.when(z < half)(far_copy(piece).wait_send))
     w_back = full.at[ROW_GRU : ROW_GRU + GATES]
     pre, inputs, raw = r.pre, r.inputs, r.raw
     low, work = r.low, r.work
@@ -360,7 +366,7 @@
         active = elu(value).astype(BF16)
         inputs[block] = active
         raw[block] = dot(active, w_gru[0:DET])
-        gather_tick(first_ticks + k)
+        pl.when(z < half)(lambda: gather_tick(first_ticks + k))
 
     pre_blocks = (horizon - 1) // 5
     each(0, pre_blocks, pre_step)
@@ -426,6 +432,10 @@
     gain = as_row(r.gain)
     bias = as_row(r.bias)
     update_ref, inv_ref = r.update, r.inv
+
+    each(0, chunks, gather_drain)
+    each(0, cuts, lambda piece: pl.when(z < half)(far_copy(piece).wait_send))
+    scan_first = first_ticks + jnp.where(z < half, pre_blocks, 0)
 
     def forward_step(t):
         block = pl.ds(mult(t * cap, 16), cap)
@@ -448,15 +458,20 @@
         w_back[pl.ds(mult(DET * k, DET), DET), pl.ds(mult(128 * j, 128), 128)] = w_gru[
             pl.ds(mult(DET + 128 * j, 128), 128), pl.ds(mult(DET * k, DET), DET)
         ].T
-        pl.when(t % 3 == 2)(lambda: gather_tick(first_ticks + pre_blocks + t // 3))
-
-    each(0, horizon - 1, forward_step)
-    done_ticks = first_ticks + pre_blocks + (horizon - 1) // 3
+
+    group = 3 if (horizon - 1) % 3 == 0 else 1
+    rounds = (horizon - 1) // group
+
+    def forward_round(m):
+        for k in range(group):
+            forward_step(m * group + k)
+        gather_tick(scan_first + m)
+
+    each(0, rounds, forward_round)
+    done_ticks = scan_first + rounds
     each(done_ticks, jnp.maximum(ticks, done_ticks), gather_tick)
     low[steps_rows:total] = states_ref[steps_rows:total].astype(BF16)
-    each(items, 2 * items, gather_shared)
-    each(items, 2 * items, gather_drain)
-    each(0, parts, lambda piece: pl.when(z >= half)(far_copy(piece).wait_send))
+    each(chunks, 2 * chunks, gather_shared)
 
     each(1, n, lambda k: moments_landing(k).wait_recv())
     sums = moments[0]
@@ -678,9 +693,9 @@
     rs_ticks = 2 * items + LAG_Z * (bits + 1)
 
     out_grads, state_grads = r.out_grads, r.state_grads
-    r.loss_acc[...] = jnp.zeros((BLOCK, 128), F32)
+    r.loss_acc[...] = jnp.zeros((plan.block, 128), F32)
     critic_row = as_row(r.critic_head)
-    lane_id = iota((BLOCK, 128), 1)
+    lane_id = iota((plan.block, 128), 1)
 
     def net_rows(side):
         return (ROW_A1, ROW_A2) if side == 0 else (ROW_C1, ROW_C2)
@@ -690,7 +705,7 @@
 
     def net_step(k, side):
         first, second = net_rows(side)
-        block = pl.ds(mult(k * BLOCK, 64), BLOCK)
+        block = pl.ds(mult(k * plan.block, 64), plan.block)
         one = dot(low[block], full[first : first + DET]) + dot(hot[block], full[first + DET : first + DET + STOCH])
         one_low = elu(one).astype(BF16)
         work[block, net_cols(a_one_at, side)] = one_low
@@ -748,9 +763,11 @@
 
         each(0, STOCH // WIDE, latent_part)
 
-    blocks = total // BLOCK
+    blocks = total // plan.block
     each(0, blocks, lambda k: net_step(k, 0))
     net_grads(0)
+    each(chunks, 2 * chunks, gather_drain)
+    each(0, cuts, lambda piece: pl.when(z >= half)(far_copy(piece).wait_send))
     each(0, net_items, heads_rs.to_pair)
     net_step(0, 1)
     each(0, net_items, heads_rs.to_b)
@@ -768,14 +785,7 @@
     small[SM_CRITIC + 1 : SM_CRITIC + 2] = head_grad[ACTIONS : ACTIONS + 1, DET + WIDE :]
     small[SM_LOSS : SM_LOSS + 1, 0:128] = jnp.sum(r.loss_acc[...], axis=0, keepdims=True)
 
-    scan_b = 2
-
-    def heads_b(index):
-        share = -(-net_items // scan_b)
-        low_item = net_items + index * share
-        each(low_item, jnp.minimum(low_item + share, items), heads_rs.to_b)
-
-    scan_ticks = net_items + (horizon - 1) // 3 - 1
+    scan_ticks = net_items + rounds - 1
 
     gain_acc, bias_acc = r.gain_acc, r.bias_acc
     gain_acc[...] = jnp.zeros((8, GATES), F32)
@@ -822,10 +832,14 @@
         grad_low = raw_grad.astype(BF16)
         work[block, 0:GATES] = grad_low
         carry_ref[...] = carry * (1.0 - update) + dot(grad_low, w_back[...]) + state_grads[block]
-        pl.when(index < scan_b)(lambda: heads_b(index))
-        pl.when((index >= scan_b) & (index % 3 == 1))(lambda: rs_tick(net_items + index // 3 - 1))
-
-    each(0, horizon - 1, backward_step)
+
+    def backward_round(m):
+        pl.when(m == 0)(lambda: each(net_items, items, heads_rs.to_b))
+        for k in range(group):
+            backward_step(m * group + k)
+        pl.when(m > 0)(lambda: rs_tick(net_items + m - 1))
+
+    each(0, rounds, backward_round)
 
     back_begin, back_finish, back_drain = exchange(DET, r.bk_send, r.bk_recv)
     out_drain()
@@ -888,11 +902,7 @@
     small_in, scattered = r.small_in, r.scattered
     summed = small_in
     swap_small = remote(small, small_in, r.pair_sem.at[2], r.pair_sem.at[3], me, sibling)
-    swap_small.start()
-    each(ready, ready + step_ticks, rs_tick)
-    swap_small.wait()
     small_sum = small
-    small_sum[...] = small[...] + small_in[...]
 
     def eight(k):
         return pl.ds(mult(k * 8, 8), 8)
@@ -913,17 +923,28 @@
         peer = (me + n - k) % n
         return remote(summed.at[eight(peer)], summed.at[eight(peer)], r.sm_send.at[k], r.sm_recv.at[k], peer)
 
-    scattered[me] = small_sum[eight(me)]
-    each(1, n, lambda k: scatter_copy(k).start())
-    landing = max(ready + step_ticks, rs_ticks - SMALL_TICKS)
-    each(ready + step_ticks, landing, rs_tick)
-    each(1, n, lambda k: scatter_landing(k).wait_recv())
-    block_sum = scattered[0]
-    for k in range(1, n):
-        block_sum = block_sum + scattered[k]
-    summed[eight(me)] = block_sum
-    each(1, n, lambda k: summed_copy(k).start())
-    each(landing, rs_ticks, rs_tick)
+    def scatter_small():
+        swap_small.wait()
+        small_sum[...] = small[...] + small_in[...]
+        scattered[me] = small_sum[eight(me)]
+        each(1, n, lambda k: scatter_copy(k).start())
+
+    def spread_small():
+        each(1, n, lambda k: scatter_landing(k).wait_recv())
+        block_sum = scattered[0]
+        for k in range(1, n):
+            block_sum = block_sum + scattered[k]
+        summed[eight(me)] = block_sum
+        each(1, n, lambda k: summed_copy(k).start())
+
+    swap_small.start()
+    between = (SCATTER_TICKS, scatter_small), (SPREAD_TICKS, spread_small)
+    for before_end, run in between:
+        until = max(ready, rs_ticks - before_end)
+        each(ready, until, rs_tick)
+        ready = until
+        run()
+    each(ready, rs_ticks, rs_tick)
     each(0, items, heads_rs.drain)
 
     back_finish()
@@ -1049,7 +1070,7 @@
         inv=((steps_rows, 128), F32),
         out_grads=((total, 128), BF16),
         state_grads=((total, DET), F32),
-        loss_acc=((BLOCK, 128), F32),
+        loss_acc=((plan.block, 128), F32),
         grads=((4, group_rows, 128), F32),
         pair_in=((half_rows, DET), BF16),
         b_in=((2, half_rows // 2, DET), BF16),
@@ -1071,13 +1092,13 @@
         sm_send=(n,),
         sm_recv=(n,),
         pair_sem=(4,),
-        ag_recv=(n, parts),
-        sh_recv=(n, parts),
-        far_send=(parts,),
-        line_send=(line, parts, max(plan.bits - 1, 1)),
-        a_send=(line, parts),
-        b_send=(line, parts, 2),
-        sh_send=(line, parts, 4),
+        ag_recv=(n, plan.cuts),
+        sh_recv=(n, plan.cuts),
+        far_send=(plan.cuts,),
+        line_send=(line, plan.cuts, max(plan.bits - 1, 1)),
+        a_send=(line, plan.cuts),
+        b_send=(line, plan.cuts, 2),
+        sh_send=(line, plan.cuts, 4),
         pair_s=(2, half, parts),
         pair_r=(2, half, parts),
         b_s=(2, half, parts),

time: 145 us -> 142 us (0.979)
  Pallas kernels: 144 us -> 141 us
    pallas_call x1, Pallas kernels: 141 us -> 138 us  [on_device(): pl.pallas_call(functools.partial(kernel_body, plan, names), out_shape=[ja...]
where the time goes in v3:
time: 142 us
  Pallas kernels  141 us (99%)
    pallas_call x1, Pallas kernels, on_device(): pl.pallas_call(functools.partial(kernel_body, plan, names), out_shape=[ja...  138 us
    pallas_call x1, Pallas kernels, on_device(): pl.pallas_call(hand_over, out_shape=[jax.ShapeDtypeStruct(shape, F32) for...  3.03 us

profile of v3, /device:TPU:0, one launch (start us, length us, event | category | flops | bytes accessed | tf_op | source)
XLA Modules:
  0.0 142.2 jit_solution(9591177735095987465)
XLA Ops:
  1.3 137.9 %shard_map.188 = (f32[1,1]{1,0:T(1,128)}, f32[96,512]{1,0:T(8,128)}, f32[2048,128]{1,0:T(8,128)}, f32[18,512]{1,0:T(8,128)}, f32[12,128]{1,0:T(8,128)}, /*index=...) custom-call(bf16[96,512]{1,0:T(8,128)(2,1)} %refs_0_.1, s32[1,96]{1,0:T(1,128)} %bitcast.26, ...), custom_call_target="tpu_custom_call" | custom-call | tf_op jit(solution)/shard_map/pallas_call | solution.py:1115
  139.2 3.0 %shard_map.189 = (f32[1,1]{1,0:T(1,128)}, f32[96,512]{1,0:T(8,128)}, f32[2048,128]{1,0:T(8,128)}, f32[18,512]{1,0:T(8,128)}, f32[12,128]{1,0:T(8,128)}, /*index=...) custom-call(f32[1,1]{1,0:T(1,128)} %get-tuple-element.24.refs_0_, f32[96,512]{1,0:T(8,128)} %get-tuple-element.25.refs_1_, ...), custom_call_target="tpu_custom_call" | custom-call | tf_op jit(solution)/shard_map/pallas_call | solution.py:1127

commit v4 on v3

--- a/solution.py
+++ b/solution.py
@@ -132,8 +132,151 @@
     for c in range(4):
         full[own_rows, 128 * c : 128 * (c + 1)] = r.narrow[pl.ds(c, rows // 2, stride=4), :].astype(BF16)
 
+    slots = plan.slots
+    lanes = n * lane
+    tall = min(lanes, 256)
+
+    def each(low, high, body):
+        def step(k, carry):
+            body(k)
+            return carry
+
+        lax.fori_loop(low, high, step, 0)
+
+    pl.semaphore_wait(barrier, n)
+
+    def lane_rows(k):
+        return pl.ds(mult(k * lane, 16), lane)
+
+    def exchange(width, sends, recvs):
+        src, dst = r.sent, r.got
+
+        def copy(k, to, into):
+            return remote(
+                src.at[lane_rows(to), 0:width], dst.at[lane_rows(into), 0:width], sends.at[k], recvs.at[k], to
+            )
+
+        def begin():
+            dst[lane_rows(me), 0:width] = src[lane_rows(me), 0:width]
+            each(1, n, lambda k: copy(k, (me + k) % n, me).start())
+
+        def finish():
+            each(1, n, lambda k: copy(k, me, (me + n - k) % n).wait_recv())
+
+        def drain():
+            each(1, n, lambda k: copy(k, (me + k) % n, me).wait_send())
+
+        return begin, finish, drain
+
+    out_begin, out_finish, out_drain = exchange(DET + META, r.ex_send, r.ex_recv)
+    cuts = plan.cuts
+    chunks = half * cuts
+    crow = rows // 2 // cuts
+    def bit_of(value, b):
+        return (value // 2**b) % 2
+
+    def across(b):
+        return me + 4 * 2**b * (1 - 2 * bit_of(z, b))
+
+    ahead = min(AHEAD, cuts)
+
+    def item_at(i):
+        i = jnp.where(z < half, i, jnp.where(i < ahead, chunks + i, jnp.where(i < ahead + chunks, i - ahead, i)))
+        late = i // cuts
+        group = late // half
+        order = late % half
+        place = z % half
+        for b in range(bits - 1):
+            place = place + bit_of(order, b) * 2**b * (1 - 2 * bit_of(z, b))
+        return order, group * half + place, i % cuts
+
+    def full_at(shard, piece, part):
+        return full.at[pl.ds(mult(shard * rows + part * (rows // 2) + piece * crow, 16), crow)]
+
+    def gather_copy(shard, piece, send, dev):
+        view = full_at(shard, piece, core)
+        return remote(view, view, send, r.ag_recv.at[shard, piece], dev)
+
+    def share_copy(shard, piece, send, part=None):
+        view = full_at(shard, piece, core if part is None else part)
+        return remote(view, view, send, r.sh_recv.at[shard, piece], me, sibling)
+
+    def far_copy(piece):
+        return gather_copy(me, piece, r.far_send.at[piece], across(bits - 1))
+
+    def plane_sends(zi, piece):
+        mine = zi * 4 + q
+        other = zi * 4 + q_a
+        return (
+            gather_copy(mine, piece, r.a_send.at[zi, piece], a_dev),
+            gather_copy(mine, piece, r.b_send.at[zi, piece, 0], b_dev),
+            gather_copy(other, piece, r.b_send.at[zi, piece, 1], b_dev),
+        )
+
+    def line_sends(order, zi, piece):
+        return [
+            (order < 2**b, gather_copy(zi * 4 + q, piece, r.line_send.at[zi, piece, b], across(b)))
+            for b in range(bits - 1)
+        ]
+
+    def gather_line(i):
+        order, zi, piece = item_at(i)
+
+        @pl.when(zi != z)
+        def _():
+            gather_copy(zi * 4 + q, piece, r.a_send.at[zi, piece], me).wait_recv()
+
+        for need, copy in line_sends(order, zi, piece):
+            pl.when(need)(copy.start)
+        to_a, to_b, _ = plane_sends(zi, piece)
+        to_a.start()
+        to_b.start()
+        share_copy(zi * 4 + q, piece, r.sh_send.at[zi, piece, 0]).start()
+
+    def gather_a(i):
+        _, zi, piece = item_at(i)
+        gather_copy(zi * 4 + q_a, piece, r.a_send.at[zi, piece], me).wait_recv()
+        plane_sends(zi, piece)[2].start()
+        share_copy(zi * 4 + q_a, piece, r.sh_send.at[zi, piece, 1]).start()
+
+    def gather_b(i):
+        _, zi, piece = item_at(i)
+        for k, where in ((2, q_b), (3, q_ab)):
+            gather_copy(zi * 4 + where, piece, r.a_send.at[zi, piece], me).wait_recv()
+            share_copy(zi * 4 + where, piece, r.sh_send.at[zi, piece, k]).start()
+
+    def gather_shared(i):
+        zi, piece = i // cuts, i % cuts
+        for k, where in ((0, q), (1, q_a), (2, q_b), (3, q_ab)):
+            share_copy(zi * 4 + where, piece, r.sh_send.at[zi, piece, k], sibling).wait_recv()
+
+    def gather_drain(i):
+        zi, piece = i // cuts, i % cuts
+        place, order = zi % half, 0
+        for b in range(bits - 1):
+            order = order + 2**b * ((bit_of(place, b) + bit_of(z, b)) % 2)
+        for need, copy in line_sends(order, zi, piece):
+            pl.when(need)(copy.wait_send)
+        for copy in plane_sends(zi, piece):
+            copy.wait_send()
+        for k, where in ((0, q), (1, q_a), (2, q_b), (3, q_ab)):
+            share_copy(zi * 4 + where, piece, r.sh_send.at[zi, piece, k]).wait_send()
+
+    lag_a, lag_b = LAG_A, LAG_B
+    all_chunks = 2 * chunks
+    ticks = all_chunks + lag_b
+    first_ticks = chunks + lag_b + jnp.where(z < half, 0, ahead)
+
+    def gather_tick(k):
+        pl.when(k < all_chunks)(lambda: gather_line(k))
+        pl.when((k >= lag_a) & (k < all_chunks + lag_a))(lambda: gather_a(k - lag_a))
+        pl.when((k >= lag_b) & (k < all_chunks + lag_b))(lambda: gather_b(k - lag_b))
+
+    each(0, cuts, lambda piece: far_copy(piece).start())
+    early = min(2, START_TICKS, chunks)
+    each(0, early, gather_tick)
+
     route = r.route[...].astype(F32)
-    slots = plan.slots
     used_row = (iota((1, slots), 1) < r.counts[...]).astype(F32)
     target_row = jnp.floor((route + 0.5) * (1.0 / cap))
     within_row = route - cap * target_row
@@ -144,15 +287,6 @@
     same = jnp.where(earlier & (target_col == target_row), used_col, 0.0)
     rank_row = jnp.sum(same, axis=0, keepdims=True)
     column_row = jnp.where(used_row > 0, target_row * lane + rank_row, -1.0)
-    lanes = n * lane
-    tall = min(lanes, 256)
-
-    def each(low, high, body):
-        def step(k, carry):
-            body(k)
-            return carry
-
-        lax.fori_loop(low, high, step, 0)
 
     def to_lanes(k):
         block = pl.ds(mult(k * tall, 16), tall)
@@ -170,138 +304,6 @@
 
     each(0, lanes // tall, to_lanes)
 
-    pl.semaphore_wait(barrier, n)
-
-    def lane_rows(k):
-        return pl.ds(mult(k * lane, 16), lane)
-
-    def exchange(width, sends, recvs):
-        src, dst = r.sent, r.got
-
-        def copy(k, to, into):
-            return remote(
-                src.at[lane_rows(to), 0:width], dst.at[lane_rows(into), 0:width], sends.at[k], recvs.at[k], to
-            )
-
-        def begin():
-            dst[lane_rows(me), 0:width] = src[lane_rows(me), 0:width]
-            each(1, n, lambda k: copy(k, (me + k) % n, me).start())
-
-        def finish():
-            each(1, n, lambda k: copy(k, me, (me + n - k) % n).wait_recv())
-
-        def drain():
-            each(1, n, lambda k: copy(k, (me + k) % n, me).wait_send())
-
-        return begin, finish, drain
-
-    out_begin, out_finish, out_drain = exchange(DET + META, r.ex_send, r.ex_recv)
-    cuts = plan.cuts
-    chunks = half * cuts
-    crow = rows // 2 // cuts
-    def bit_of(value, b):
-        return (value // 2**b) % 2
-
-    def across(b):
-        return me + 4 * 2**b * (1 - 2 * bit_of(z, b))
-
-    ahead = min(AHEAD, cuts)
-
-    def item_at(i):
-        i = jnp.where(z < half, i, jnp.where(i < ahead, chunks + i, jnp.where(i < ahead + chunks, i - ahead, i)))
-        late = i // cuts
-        group = late // half
-        order = late % half
-        place = z % half
-        for b in range(bits - 1):
-            place = place + bit_of(order, b) * 2**b * (1 - 2 * bit_of(z, b))
-        return order, group * half + place, i % cuts
-
-    def full_at(shard, piece, part):
-        return full.at[pl.ds(mult(shard * rows + part * (rows // 2) + piece * crow, 16), crow)]
-
-    def gather_copy(shard, piece, send, dev):
-        view = full_at(shard, piece, core)
-        return remote(view, view, send, r.ag_recv.at[shard, piece], dev)
-
-    def share_copy(shard, piece, send, part=None):
-        view = full_at(shard, piece, core if part is None else part)
-        return remote(view, view, send, r.sh_recv.at[shard, piece], me, sibling)
-
-    def far_copy(piece):
-        return gather_copy(me, piece, r.far_send.at[piece], across(bits - 1))
-
-    def plane_sends(zi, piece):
-        mine = zi * 4 + q
-        other = zi * 4 + q_a
-        return (
-            gather_copy(mine, piece, r.a_send.at[zi, piece], a_dev),
-            gather_copy(mine, piece, r.b_send.at[zi, piece, 0], b_dev),
-            gather_copy(other, piece, r.b_send.at[zi, piece, 1], b_dev),
-        )
-
-    def line_sends(order, zi, piece):
-        return [
-            (order < 2**b, gather_copy(zi * 4 + q, piece, r.line_send.at[zi, piece, b], across(b)))
-            for b in range(bits - 1)
-        ]
-
-    def gather_line(i):
-        order, zi, piece = item_at(i)
-
-        @pl.when(zi != z)
-        def _():
-            gather_copy(zi * 4 + q, piece, r.a_send.at[zi, piece], me).wait_recv()
-
-        for need, copy in line_sends(order, zi, piece):
-            pl.when(need)(copy.start)
-        to_a, to_b, _ = plane_sends(zi, piece)
-        to_a.start()
-        to_b.start()
-        share_copy(zi * 4 + q, piece, r.sh_send.at[zi, piece, 0]).start()
-
-    def gather_a(i):
-        _, zi, piece = item_at(i)
-        gather_copy(zi * 4 + q_a, piece, r.a_send.at[zi, piece], me).wait_recv()
-        plane_sends(zi, piece)[2].start()
-        share_copy(zi * 4 + q_a, piece, r.sh_send.at[zi, piece, 1]).start()
-
-    def gather_b(i):
-        _, zi, piece = item_at(i)
-        for k, where in ((2, q_b), (3, q_ab)):
-            gather_copy(zi * 4 + where, piece, r.a_send.at[zi, piece], me).wait_recv()
-            share_copy(zi * 4 + where, piece, r.sh_send.at[zi, piece, k]).start()
-
-    def gather_shared(i):
-        zi, piece = i // cuts, i % cuts
-        for k, where in ((0, q), (1, q_a), (2, q_b), (3, q_ab)):
-            share_copy(zi * 4 + where, piece, r.sh_send.at[zi, piece, k], sibling).wait_recv()
-
-    def gather_drain(i):
-        zi, piece = i // cuts, i % cuts
-        place, order = zi % half, 0
-        for b in range(bits - 1):
-            order = order + 2**b * ((bit_of(place, b) + bit_of(z, b)) % 2)
-        for need, copy in line_sends(order, zi, piece):
-            pl.when(need)(copy.wait_send)
-        for copy in plane_sends(zi, piece):
-            copy.wait_send()
-        for k, where in ((0, q), (1, q_a), (2, q_b), (3, q_ab)):
-            share_copy(zi * 4 + where, piece, r.sh_send.at[zi, piece, k]).wait_send()
-
-    lag_a, lag_b = LAG_A, LAG_B
-    all_chunks = 2 * chunks
-    ticks = all_chunks + lag_b
-    first_ticks = chunks + lag_b + jnp.where(z < half, 0, ahead)
-
-    def gather_tick(k):
-        pl.when(k < all_chunks)(lambda: gather_line(k))
-        pl.when((k >= lag_a) & (k < all_chunks + lag_a))(lambda: gather_a(k - lag_a))
-        pl.when((k >= lag_b) & (k < all_chunks + lag_b))(lambda: gather_b(k - lag_b))
-
-    each(0, cuts, lambda piece: far_copy(piece).start())
-    early = min(2, START_TICKS, chunks)
-    each(0, early, gather_tick)
 
     hot, hot_t, act_hot = r.hot, r.hot_t, r.act_hot
     for t in range(horizon):
@@ -412,8 +414,6 @@
     pair[0] = sums
     swap = remote(pair.at[0], pair.at[1], r.pair_sem.at[0], r.pair_sem.at[1], me, sibling)
     swap.start()
-    swap.wait()
-    moments[me] = pair[0] + pair[1]
 
     def moments_copy(k):
         peer = (me + k) % n
@@ -423,7 +423,6 @@
         peer = (me + n - k) % n
         return remote(moments.at[peer], moments.at[peer], r.mo_send.at[k], r.mo_recv.at[k], peer)
 
-    each(1, n, lambda k: moments_copy(k).start())
 
     def as_row(ref):
         value = ref[...].astype(F32)
@@ -467,12 +466,11 @@
             forward_step(m * group + k)
         gather_tick(scan_first + m)
 
-    each(0, rounds, forward_round)
-    done_ticks = scan_first + rounds
-    each(done_ticks, jnp.maximum(ticks, done_ticks), gather_tick)
-    low[steps_rows:total] = states_ref[steps_rows:total].astype(BF16)
-    each(chunks, 2 * chunks, gather_shared)
-
+    each(0, 1, forward_round)
+    swap.wait()
+    moments[me] = pair[0] + pair[1]
+    each(1, n, lambda k: moments_copy(k).start())
+    each(1, rounds, forward_round)
     each(1, n, lambda k: moments_landing(k).wait_recv())
     sums = moments[0]
     for k in range(1, n):
@@ -483,6 +481,11 @@
         [(r.returns[...] - centre) / spread, r.weight_row[...], jnp.zeros((126, total), F32)], axis=0
     ).T
     adv[...] = per_row
+
+    done_ticks = scan_first + rounds
+    each(done_ticks, jnp.maximum(ticks, done_ticks), gather_tick)
+    low[steps_rows:total] = states_ref[steps_rows:total].astype(BF16)
+    each(chunks, 2 * chunks, gather_shared)
 
     grads = r.grads
 

time: 142 us -> 141 us (level)
  no operation moved by 1% of the time
where the time goes in v4:
time: 141 us
  Pallas kernels  140 us (99%)
    pallas_call x1, Pallas kernels, on_device(): pl.pallas_call(functools.partial(kernel_body, plan, names), out_shape=[ja...  137 us
    pallas_call x1, Pallas kernels, on_device(): pl.pallas_call(hand_over, out_shape=[jax.ShapeDtypeStruct(shape, F32) for...  3.03 us

profile of v4, /device:TPU:0, one launch (start us, length us, event | category | flops | bytes accessed | tf_op | source)
XLA Modules:
  0.0 140.8 jit_solution(4365503331925079213)
XLA Ops:
  1.3 136.5 %shard_map.188 = (f32[1,1]{1,0:T(1,128)}, f32[96,512]{1,0:T(8,128)}, f32[2048,128]{1,0:T(8,128)}, f32[18,512]{1,0:T(8,128)}, f32[12,128]{1,0:T(8,128)}, /*index=...) custom-call(bf16[96,512]{1,0:T(8,128)(2,1)} %refs_0_.1, s32[1,96]{1,0:T(1,128)} %bitcast.26, ...), custom_call_target="tpu_custom_call" | custom-call | tf_op jit(solution)/shard_map/pallas_call | solution.py:1118
  137.8 3.0 %shard_map.189 = (f32[1,1]{1,0:T(1,128)}, f32[96,512]{1,0:T(8,128)}, f32[2048,128]{1,0:T(8,128)}, f32[18,512]{1,0:T(8,128)}, f32[12,128]{1,0:T(8,128)}, /*index=...) custom-call(f32[1,1]{1,0:T(1,128)} %get-tuple-element.24.refs_0_, f32[96,512]{1,0:T(8,128)} %get-tuple-element.25.refs_1_, ...), custom_call_target="tpu_custom_call" | custom-call | tf_op jit(solution)/shard_map/pallas_call | solution.py:1130
